TPU v7x, 512 devices: a whole 4x8x8 slice. The times are simulated.
512 devices in a mesh: img: 64 (over y, z_hi, x), vol: 8 (over z_lo, core).
Axes of the slice: x: 4, y: 8, z: 8 (z_hi: 2, z_lo: 4; z = z_hi * 4 + z_lo), core: 2. Of those that a mesh axis runs over, the one named last changes fastest.
Arguments:
- images: bfloat16 [2048, 256, 256], P('img', 'vol'), may hold values from -6 to 6
- volume: bfloat16 [8, 256, 256], P(None, 'vol'), may hold values from -6 to 6
- ctf_table: float32 [16, 256, 128], P(None, 'vol'), may hold values from -1 to 1
- ctf_class: int32 [2048], P('img'), may hold values from 0 to 15
- pose_list: int32 [2048, 32], P('img'), may hold values from 0 to 63, as said below
- tilt: float32 [64], replicated, may hold values from -0.03 to 0.03
- offset: float32 [64], replicated, may hold values from 2 to 5
- magnif: float32 [64], replicated, may hold values from 0.92 to 1.08
- noise_inverse: float32 [2048], P('img'), may hold values from 0.009765625 to 0.09765625
- prior: float32 [8, 256, 128], P(None, 'vol'), may hold values from 0.005 to 0.05
Outputs:
- weights: float32 [2048, 32], P('img')
- planes: float32 [8, 256, 256], P('vol')
Inputs may be any that keep to these rules, and one draw needn't show every extreme that they name: `pose_list`: each image lists 32 different poses.
All inputs are finite; a program needn't handle non-finite values.
Results may differ from a plain program's by a relative error of at most 0.002.
Values may be sent and summed in bfloat16 or wider, within the bound.
A program may use at most 64 MiB of HBM per device.

v0:
```python
import jax
import jax.numpy as jnp
from jax import lax
from jax.sharding import PartitionSpec as P


def pose_tables(tilt, offset, magnif, cols, depth_count):
    columns = jnp.arange(cols, dtype=jnp.float32)
    sample_x = (magnif * jnp.cos(tilt))[:, None] * columns[None, :]
    sample_z = offset[:, None] + jnp.sin(tilt)[:, None] * columns[None, :]
    across = jnp.maximum(0.0, 1.0 - jnp.abs(columns[None, :, None] - sample_x[:, None, :])).astype(
        jnp.bfloat16
    )
    levels = jnp.arange(depth_count, dtype=jnp.float32)
    depth = jnp.maximum(0.0, 1.0 - jnp.abs(levels[None, :, None] - sample_z[:, None, :]))
    return (across, depth)


def row_transform(fresh):
    rows = jnp.arange(fresh.shape[2], dtype=jnp.int32)
    phase = rows[:, None] * rows[None, :] % fresh.shape[2]
    angle = phase.astype(jnp.float32) * (2.0 * jnp.pi / fresh.shape[2])
    cosine = jnp.cos(angle)
    sine = jnp.sin(angle)
    even = jnp.einsum("ky,zcyx->zckx", cosine, fresh, precision=lax.Precision.HIGHEST)
    odd = jnp.einsum("ky,zcyx->zckx", sine, fresh, precision=lax.Precision.HIGHEST)
    real_part = even[:, 0] + odd[:, 1]
    imag_part = even[:, 1] - odd[:, 0]
    return jnp.concatenate([real_part, imag_part], axis=2)


def project(volume, across, depth):
    levels, rows, width = volume.shape
    cols = width // 2
    total = across.shape[0]
    flat = volume.reshape(levels * rows * 2, cols)
    pieces = []
    for begin in range(0, total, 8):
        stop = min(total, begin + 8)
        size = stop - begin
        table = jnp.transpose(across[begin:stop], (1, 0, 2)).reshape(cols, size * cols)
        spread = jnp.dot(flat, table, preferred_element_type=jnp.float32).reshape(
            levels, rows * 2, size, cols
        )
        weight = jnp.transpose(depth[begin:stop], (1, 0, 2))[:, None, :, :]
        summed = jnp.sum(spread * weight, axis=0)
        pieces.append(jnp.transpose(summed, (1, 0, 2)).astype(jnp.bfloat16))
    joined = jnp.concatenate(pieces, axis=0)
    return joined.reshape(total, rows, width)


def back_project(stacked, across, depth):
    total, rows, width = stacked.shape
    cols = width // 3
    levels = depth.shape[1]
    result = jnp.zeros((levels, 3, rows, cols), jnp.float32)
    for begin in range(0, total, 8):
        stop = min(total, begin + 8)
        block = stacked[begin:stop]
        part = jnp.stack(
            [block[:, :, 0:cols], block[:, :, cols : 2 * cols], block[:, :, 2 * cols : 3 * cols]],
            axis=1,
        ).astype(jnp.float32)
        spread = (depth[begin:stop][:, :, None, None, :] * part[:, None]).astype(jnp.bfloat16)
        result = result + lax.dot_general(
            spread,
            across[begin:stop],
            (((0, 4), (0, 2)), ((), ())),
            preferred_element_type=jnp.float32,
        )
    return result


def per_device(
    images, volume, ctf_table, ctf_class, pose_list, tilt, offset, magnif, noise_inverse, prior
):
    highest = lax.Precision.HIGHEST
    count, rows, width = images.shape
    cols = width // 2
    levels = volume.shape[0]
    poses = tilt.shape[0]
    classes = ctf_table.shape[0]
    across, depth = pose_tables(tilt, offset, magnif, cols, levels)
    slices = project(volume, across, depth)
    class_hot = (ctf_class[:, None] == jnp.arange(classes, dtype=jnp.int32)[None, :]).astype(
        jnp.float32
    )
    ctf_own = jnp.dot(class_hot, ctf_table.reshape(classes, -1), precision=highest).reshape(
        count, rows, cols
    )
    ctf_both = jnp.concatenate([ctf_own, ctf_own], axis=2)
    filtered = (images.astype(jnp.float32) * ctf_both).astype(jnp.bfloat16).reshape(count, -1)
    cross = lax.dot_general(
        filtered,
        slices.reshape(poses, -1),
        (((1,), (1,)), ((), ())),
        preferred_element_type=jnp.float32,
    )
    sliced = slices.astype(jnp.float32)
    power = sliced[:, :, 0:cols] * sliced[:, :, 0:cols] + sliced[:, :, cols:] * sliced[:, :, cols:]
    ctf_sq = ctf_table * ctf_table
    norm = lax.dot_general(
        ctf_sq.reshape(classes, -1),
        power.reshape(poses, -1),
        (((1,), (1,)), ((), ())),
        precision=highest,
    )
    norm_img = jnp.sum(class_hot[:, :, None] * norm[None, :, :], axis=1)
    poses_hot = (pose_list[:, :, None] == jnp.arange(poses, dtype=jnp.int32)[None, None, :]).astype(
        jnp.float32
    )
    partial_value = jnp.sum(poses_hot * (cross - 0.5 * norm_img)[:, None, :], axis=2)
    distance = lax.psum(partial_value, "vol")
    weights = jax.nn.softmax(noise_inverse[:, None] * distance, axis=1)
    resp = jnp.sum(weights[:, :, None] * poses_hot, axis=1).astype(jnp.bfloat16)
    counts = lax.dot_general(
        resp.astype(jnp.float32), class_hot, (((0,), (0,)), ((), ())), precision=highest
    )
    sums = lax.dot_general(
        resp, filtered, (((0,), (0,)), ((), ())), preferred_element_type=jnp.float32
    )
    stacked = lax.psum(
        jnp.concatenate(
            [
                sums.reshape(poses, rows, 2 * cols),
                jnp.dot(counts, ctf_sq.reshape(classes, -1), precision=highest).reshape(
                    poses, rows, cols
                ),
            ],
            axis=2,
        ),
        "img",
    ).astype(jnp.bfloat16)
    volume_sum = back_project(stacked, across, depth)
    images_all = float(count * lax.axis_size("img"))
    fresh = volume_sum[:, 0:2] / (volume_sum[:, 2:3] + images_all * prior[:, None])
    turned = lax.all_to_all(fresh, "vol", split_axis=0, concat_axis=2, tiled=True)
    planes = row_transform(turned)
    return (weights, planes)


def solution(mesh):
    placed = (
        P("img", "vol", None),
        P(None, "vol", None),
        P(None, "vol", None),
        P("img"),
        P("img", None),
        P(),
        P(),
        P(),
        P("img"),
        P(None, "vol", None),
    )
    return jax.shard_map(
        per_device,
        mesh=mesh,
        in_specs=placed,
        out_specs=(P("img", None), P("vol", None, None)),
        check_vma=False,
    )
```

profile of v0, /device:TPU:1, one launch (start us, length us, event | category | flops | bytes accessed | tf_op | source)
XLA Modules:
  0.0 634.9 jit_solution(2580395354826369566)
XLA Ops:
  6.1 1.8 copy.110
  7.9 2.1 copy.168
  14.0 1.8 copy.112
  15.9 2.1 copy.169
  17.9 1.8 copy.113
  19.7 2.7 convolution_bitcast_fusion.5
  22.4 2.9 copy.114
  25.3 3.4 copy.170
  28.7 1.8 copy.115
  30.5 2.7 convolution_bitcast_fusion.4
  33.2 2.9 copy.116
  36.1 3.4 copy.171
  39.5 1.8 copy.117
  41.3 2.7 convolution_bitcast_fusion.3
  44.0 3.0 copy.118
  47.0 3.4 copy.172
  50.4 1.8 copy.119
  52.2 2.8 convolution_bitcast_fusion.2
  55.0 2.9 copy.120
  57.9 3.4 copy.173
  61.3 1.8 copy.121
  63.1 2.7 convolution_bitcast_fusion.1
  65.8 2.9 copy.122
  68.7 3.4 copy.174
  72.9 2.7 convolution_bitcast_fusion
  75.6 2.9 copy.124
  78.6 2.1 copy.175
  86.1 1.9 copy.127
  88.0 1.9 reshape.437
  95.5 28.7 %psum.14 = f32[32,32]{1,0:T(8,128)S(1)} all-reduce(f32[32,32]{1,0:T(8,128)S(1)} %select_reduce_fusion.1), channel_id=1, replica_groups=mesh['img'=64,'vol'=8] {'vol'}, use_global_device_ids=true, to_apply=%region_10.0 | all-reduce | flops 1024 | bytes 8192 | tf_op jit(solution)/shard_map/psum | solution.py:113
  127.0 432.0 %all-reduce.1 = bf16[64,32,384]{2,0,1:T(8,128)(2,1)} all-reduce(f32[64,32,384]{2,0,1:T(8,128)S(1)} %pad_maximum_fusion), channel_id=1, replica_groups=mesh['img'=64,'vol'=8] {'img'}, use_global_device_ids=true, to_apply=%region_14.0 | all-reduce | flops 786432 | bytes 4718592 | tf_op jit(solution)/shard_map/psum | solution.py:122
  568.5 62.5 %all_to_all.15 = f32[8,2,32,128]{3,2,1,0:T(8,128)S(1)} all-to-all(f32[8,2,32,128]{3,2,1,0:T(8,128)S(1)} %slice_divide_fusion), channel_id=1, replica_groups=mesh['img'=64,'vol'=8] {'vol'}, dimensions={0} | all-to-all | bytes 524288 | tf_op jit(solution)/shard_map/all_to_all | solution.py:137
  (147 shorter events, 36.9 us)
Async XLA Ops:
  2.9 1.4 copy-start
  4.3 1.4 copy-start.20
  78.6 2.1 copy-start.18
  80.6 1.6 copy-start.2
  80.6 1.6 copy-start.17
  80.7 2.2 copy-start.3
  80.7 2.2 copy-start.16
  82.2 1.8 copy-start.4
  82.2 1.8 copy-start.15
  82.9 1.7 copy-start.5
  82.9 1.7 copy-start.14
  84.0 1.7 copy-start.6
  84.0 1.7 copy-start.13
  84.6 1.3 copy-start.12
  86.1 1.9 copy-start.9
  89.9 1.0 copy-start.7
  89.9 1.0 copy-start.32
  91.5 3.2 copy-start.10
  93.0 2.1 copy-start.21
  93.0 31.2 %copy-start.31 = (f32[32]{0:T(128)S(1)}, f32[32]{0:T(128)}, u32[]{:S(2)}) copy-start(f32[32]{0:T(128)} %param.18) | copy-start | bytes 388
  93.0 32.0 %copy-start.8 = (bf16[32,32,256]{2,1,0:T(8,128)(2,1)S(1)}, bf16[32,32,256]{2,1,0:T(8,128)(2,1)}, u32[]{:S(2)}) copy-start(bf16[32,32,256]{2,1,0:T(8,128)(2,1)} %param.10) | copy-start | bytes 1572868
  124.7 2.1 copy-start.22
  562.1 1.6 copy-start.1
  562.1 1.6 copy-start.30
  562.3 2.0 copy-start.29
  562.5 2.4 copy-start.28
  564.3 1.2 copy-start.27
  564.9 1.2 copy-start.26
  565.5 1.2 copy-start.25
  566.1 1.2 copy-start.24
  566.7 1.2 copy-start.23
  567.3 1.2 copy-start.19
  (1 other events, 1.0 us)
where the time goes:
time: 636 us; the launch traced here: 635 us
  blocking collectives  523 us (82%)
  local copies, waits for them, and re-layouts  73.5 us (12%)
  matrix products  29.7 us (5%)
  other arithmetic  7.11 us (1%)
    psum x1, blocking collectives, per_device(): lax.psum(jnp.concatenate([sums.reshape(poses, rows, 2 * cols), jnp.dot(co...  432 us
    all_to_all x1, blocking collectives, per_device(): lax.all_to_all(fresh, 'vol', split_axis=0, concat_axis=2, tiled=True)  62.5 us
    unnamed x82, local copies, waits for them, and re-layouts  32.5 us
    psum x1, blocking collectives, per_device(): distance = lax.psum(partial_value, 'vol')  28.7 us
    dot_general x8, local copies, waits for them, and re-layouts, project(): jnp.dot(flat, table, preferred_element_type=jnp.float32)  21.1 us
    dot_general x8, matrix products, project(): jnp.dot(flat, table, preferred_element_type=jnp.float32)  18.1 us

commit v1 on v0

v1 whole, which is shorter than its diff:
```python
import functools
import jax
import jax.numpy as jnp
import numpy as np
from jax import lax
from jax.experimental import pallas as pl
from jax.experimental.pallas import tpu as pltpu
from jax.sharding import PartitionSpec as P

NY = 8
NG = 16
NX = 4
NV = 8
F32 = jnp.float32
BF16 = jnp.bfloat16
CODE = jnp.int16
STEPS, FLOOR = 982.0, 27.73
NT = (((1,), (1,)), ((), ()))


def dft_table():
    y = np.arange(256).reshape(16, 16)
    phase = (np.arange(256)[:, None, None] * y[None]) % 256
    angle = phase * (2.0 * np.pi / 256)
    cosine, sine = np.cos(angle), np.sin(angle)
    real = np.stack([cosine, sine], axis=2).reshape(256, 512)
    imag = np.stack([-sine, cosine], axis=2).reshape(256, 512)
    full = np.concatenate([real, imag], axis=0).astype(np.float32)
    return full


def split(x):
    high = x.astype(BF16)
    return high, (x - high.astype(F32)).astype(BF16)


def row_to_col(row, n):
    eye = lax.broadcasted_iota(jnp.int32, (n, n), 0) == lax.broadcasted_iota(jnp.int32, (n, n), 1)
    return jnp.sum(jnp.where(eye, row, 0.0), axis=1, keepdims=True)


def encode(rows):
    level = jnp.log(jnp.maximum(jnp.abs(rows), 1e-12)) + FLOOR
    level = jnp.round(jnp.clip(level, 0.0, 32.73) * STEPS)
    return jnp.where(rows < 0.0, -level, level).astype(jnp.int32).astype(CODE)


def decode(code):
    level = code.astype(jnp.int32).astype(F32)
    value = jnp.exp(jnp.abs(level) * (1.0 / STEPS) - FLOOR)
    return jnp.where(level < 0.0, -value, value)


def cat(parts, axis):
    return jnp.concatenate(parts, axis=axis)


def kernel(
    images_all,
    tilt_h, offset_h, magnif_h, volume_h, images_h, ctf_h, cls_h, cls_row_h, poses_h, noise_h, prior_h,
    w_out, gq,
    tilt_v, offset_v, magnif_v, volume, images, ctf, cls_s, cls_v, poses_v, noise_v, prior,
    ap, sx, depth, ctfy, tab, sl, fil, sums, sw,
    dbuf, cabuf, cbbuf, vout, own, abuf, xbuf, fref,
    load_sem, d_s, d_r, ca_s, ca_r, cb_s, cb_r, a_s, a_r, b_s, b_r, e_s, e_r,
):
    img, vol = lax.axis_index("img"), lax.axis_index("vol")
    g, x = lax.div(img, NX), lax.rem(img, NX)
    a, half = lax.div(g, 2), lax.rem(g, 2)

    loads = [
        pltpu.make_async_copy(src, dst, load_sem.at[n])
        for n, (src, dst) in enumerate(
            [
                (tilt_h, tilt_v), (offset_h, offset_v), (magnif_h, magnif_v), (volume_h, volume),
                (images_h, images), (ctf_h, ctf), (cls_h, cls_s), (cls_row_h, cls_v),
                (poses_h, poses_v), (noise_h, noise_v), (prior_h, prior),
            ]
        )
    ]
    for load in loads:
        load.start()

    def vol_peer(k):
        return (img, lax.rem(vol + k, NV))

    def g_index(k):
        n = k // 2
        m = (n + 1) // 2
        offset = 4 + m * (1 - 2 * (n % 2))
        return lax.rem(a + offset, NY) * 2 + lax.rem(half + 1 - k % 2, 2)

    def each(count, act, start=0):
        def step(k, carry):
            act(k)
            return carry

        lax.fori_loop(start, count, step, 0)

    def g_peer(t):
        return (t * NX + x, vol)

    def x_peer(t):
        return (g * NX + t, vol)

    barrier = pltpu.get_barrier_semaphore()

    def greet(dev):
        pl.semaphore_signal(barrier, inc=1, device_id=dev, device_id_type=pl.DeviceIdType.MESH)

    each(NV, lambda k: greet(vol_peer(k)), 1)
    each(NX, lambda k: greet(x_peer(lax.rem(x + k, NX))), 1)
    each(NG - 1, lambda k: greet(g_peer(g_index(k))))
    mine = a == 0
    plane = lax.rem(a + vol, NV)

    def source(t):
        return (t * NX + x, lax.rem(vol + NV - lax.div(t, 2), NV))

    each(NG - 1, lambda k: greet(source(g_index(k))))

    @pl.when(jnp.logical_not(mine))
    def _():
        greet(source(g))

    def remote(src, dst, ss, rs, dev):
        return pltpu.make_async_remote_copy(
            src_ref=src, dst_ref=dst, send_sem=ss, recv_sem=rs, device_id=dev,
            device_id_type=pl.DeviceIdType.MESH,
        )

    for load in loads[0:3]:
        load.wait()
    lanes = lax.broadcasted_iota(jnp.int32, (64, 128), 1).astype(F32)
    tilt = tilt_v[...]
    ap[...] = jnp.broadcast_to(row_to_col(magnif_v[...] * jnp.cos(tilt), 64), (64, 128))
    sx[...] = ap[...] * lanes
    sz = row_to_col(offset_v[...], 64) + row_to_col(jnp.sin(tilt), 64) * lanes
    for z in range(8):
        depth[z * 64 : (z + 1) * 64, :] = jnp.maximum(0.0, 1.0 - jnp.abs(float(z) - sz))

    loads[3].wait()

    def project_pair(j):
        xs = lax.broadcasted_iota(jnp.int32, (128, 128), 0).astype(F32)
        halves = [
            jnp.maximum(0.0, 1.0 - jnp.abs(xs - sx[pl.ds(2 * j + h, 1), :])).astype(BF16)
            for h in range(2)
        ]
        table = cat(halves, 1)
        dz = [
            cat([depth[pl.ds(z * 64 + 2 * j + h, 1), :] for h in range(2)], 1) for z in range(8)
        ]
        even_w = (dz[0] + dz[2]) + (dz[4] + dz[6])
        odd_w = (dz[1] + dz[3]) + (dz[5] + dz[7])
        on = [jnp.broadcast_to(d, (32, 256)) > 0.0 for d in dz[:6]]
        for c in range(2):
            flat = volume[:, :, c * 128 : (c + 1) * 128].reshape(256, 128)
            spread = jnp.dot(flat, table, preferred_element_type=F32)
            s = [spread[z * 32 : (z + 1) * 32, :] for z in range(8)]
            even = jnp.where(on[0], s[0], jnp.where(on[2], s[2], jnp.where(on[4], s[4], s[6])))
            odd = jnp.where(on[1], s[1], jnp.where(on[3], s[3], jnp.where(on[5], s[5], s[7])))
            slab = (even * even_w + odd * odd_w).astype(BF16).astype(F32)
            for h in range(2):
                sl[c, pl.ds(2 * j + h, 32, stride=64), :] = slab[:, h * 128 : (h + 1) * 128]

    def project(t, carry):
        for n in range(4):
            project_pair(t * 4 + n)
        return carry

    lax.fori_loop(0, 8, project, 0)

    for load in loads[4:10]:
        load.wait()

    def filtering(t, carry):
        for n in range(8):
            i = t * 8 + n
            own = ctf[cls_s[i]]
            for c in range(2):
                f = images[i, :, c * 128 : (c + 1) * 128].astype(F32) * own
                fil[c, pl.ds(i, 32, stride=32), :] = f.astype(BF16).astype(F32)
        return carry

    lax.fori_loop(0, 4, filtering, 0)
    for k in range(16):
        ctfy[pl.ds(k, 32, stride=16), :] = ctf[k]

    def scoring(g, carry):
        cross, norm = carry
        lhs, rhs, nl, nr = [], [], [], []
        for n in range(8):
            y = g * 8 + n
            power = None
            for c in range(2):
                lhs.append(fil[c, pl.ds(pl.multiple_of(y * 32, 32), 32), :].astype(BF16))
                s = sl[c, pl.ds(pl.multiple_of(y * 64, 64), 64), :]
                rhs.append(s.astype(BF16))
                power = s * s if power is None else power + s * s
            t = ctfy[pl.ds(pl.multiple_of(y * 16, 16), 16), :]
            th, tl = split(t * t)
            ph, plo = split(power)
            nl += [th, tl, th]
            nr += [ph, ph, plo]
        cross = cross + lax.dot_general(cat(rhs, 1), cat(lhs, 1), NT, preferred_element_type=F32)
        norm = norm + lax.dot_general(cat(nr, 1), cat(nl, 1), NT, preferred_element_type=F32)
        return cross, norm

    cross, norm = lax.fori_loop(
        0, 4, scoring, (jnp.zeros((64, 32), F32), jnp.zeros((64, 16), F32))
    )
    hot = (lax.broadcasted_iota(jnp.int32, (16, 32), 0) == cls_v[...]).astype(F32).astype(BF16)
    n1 = norm.astype(BF16)
    n2, n3 = split(norm - n1.astype(F32))
    norm_img = jnp.dot(cat([n1, n2, n3], 1), cat([hot, hot, hot], 0), preferred_element_type=F32)
    part = cross - 0.5 * norm_img
    dbuf[vol] = cat([part[16 * g : 16 * g + 16] for g in range(4)], 1)

    pl.semaphore_wait(barrier, 41 - mine.astype(jnp.int32))

    def d_copy(v, k):
        return remote(dbuf.at[v], dbuf.at[v], d_s.at[k], d_r.at[v], vol_peer(k))

    each(NV, lambda k: d_copy(vol, k).start(), 1)

    def turn(t, carry):
        us = lax.broadcasted_iota(jnp.int32, (128, 128), 0).astype(F32)
        xs = lax.broadcasted_iota(jnp.int32, (128, 128), 1).astype(F32)
        for n in range(4):
            p = t * 4 + n
            at = jnp.abs(xs - ap[pl.ds(p, 1), :] * us)
            tab[pl.ds(pl.multiple_of(p * 128, 128), 128), :] = jnp.maximum(0.0, 1.0 - at).astype(BF16)
        return carry

    lax.fori_loop(0, 16, turn, 0)
    pose_t = poses_v[...].astype(F32).T
    pose_iota = lax.broadcasted_iota(jnp.int32, (64, 32), 0).astype(F32)
    listed = jnp.zeros((64, 32), F32)
    for j in range(32):
        listed = listed + jnp.where(pose_t[j : j + 1, :] == pose_iota, 1.0, 0.0)

    each(NV, lambda k: d_copy(lax.rem(vol + k, NV), k).wait_recv(), 1)
    packed = dbuf[0]
    for v in range(1, NV):
        packed = packed + dbuf[v]
    distance = cat([packed[:, 32 * g : 32 * g + 32] for g in range(4)], 0)
    logits = jnp.where(listed > 0.0, noise_v[...] * distance, -3.0e38)
    grown = jnp.exp(logits - jnp.max(logits, axis=0, keepdims=True))
    grown = jnp.where(listed > 0.0, grown, 0.0)
    resp32 = grown / jnp.sum(grown, axis=0, keepdims=True)
    resp = resp32.astype(BF16)

    counts = lax.dot_general(resp, hot, NT, preferred_element_type=F32)
    cabuf[g] = cat([counts[8 * n : 8 * n + 8] for n in range(8)], 1)
    def ca_copy(t, k):
        return remote(cabuf.at[t], cabuf.at[t], ca_s.at[k], ca_r.at[t], g_peer(g_index(k)))

    def cb_copy(t, k):
        return remote(cbbuf.at[t], cbbuf.at[t], cb_s.at[k], cb_r.at[t], x_peer(lax.rem(x + k, NX)))

    def a_copy(z, t, k, slot):
        return remote(vout.at[z, lax.rem(t, 2)], abuf.at[slot], a_s.at[k], a_r.at[slot], g_peer(t))

    def b_copy(t, k):
        return remote(xbuf.at[t], xbuf.at[t], b_s.at[k], b_r.at[t], x_peer(lax.rem(x + k, NX)))

    each(NG - 1, lambda k: ca_copy(g, k).start())

    def summing(t, carry):
        for n in range(8):
            y = t * 8 + n
            f = cat(
                [fil[c, pl.ds(pl.multiple_of(y * 32, 32), 32), :].astype(BF16) for c in range(2)],
                1,
            )
            s = jnp.dot(resp, f, preferred_element_type=F32)
            row = lax.div(t, 2) * 32 + lax.rem(t, 2) * 8 + n
            for c in range(2):
                sums[pl.ds(row + 16 * c, 64, stride=64), :] = s[:, c * 128 : (c + 1) * 128]
        return carry

    lax.fori_loop(0, 4, summing, 0)

    def back(planes):
        def body(t, acc):
            blocks = []
            for n in range(16):
                p = t * 16 + n
                s = sums[pl.ds(pl.multiple_of(p * 64, 64), 64), :]
                blocks.append(
                    cat([(s * depth[pl.ds(z * 64 + p, 1), :]).astype(BF16) for z in planes], 0)
                )
            table = tab[pl.ds(pl.multiple_of(t * 2048, 2048), 2048), :]
            return acc + jnp.dot(cat(blocks, 1), table, preferred_element_type=F32)

        return lax.fori_loop(0, 4, body, jnp.zeros((64 * len(planes), 128), F32))

    def y_plane(k):
        return lax.rem(lax.div(g_index(k), 2) + vol, NV)

    for r in range(2):
        planes = [y_plane(8 * r + 2 * n) for n in range(4)]
        acc = back(planes)
        for n, z in enumerate(planes):
            piece = acc[n * 64 : (n + 1) * 64, :].reshape(2, 32, 128)
            vout[z] = piece.astype(BF16)
            if r == 1 and n == 3:
                own[...] = piece
        each(8 * r + 8 - r, lambda k: a_copy(y_plane(k), g_index(k), k, g).start(), 8 * r)
        if r == 0:
            each(NG - 1, lambda k: ca_copy(g_index(k), k).wait_recv())
            total = cabuf[0]
            for t in range(1, NG):
                total = total + cabuf[t]
            cbbuf[x] = total
            each(NX, lambda k: cb_copy(x, k).start(), 1)

    each(NX, lambda k: cb_copy(lax.rem(x + k, NX), k).wait_recv(), 1)
    total = (cbbuf[0] + cbbuf[1]) + (cbbuf[2] + cbbuf[3])
    counts_all = cat([total[:, 16 * n : 16 * n + 16] for n in range(8)], 0)
    ch, cl = split(counts_all)
    counts3 = cat([ch, cl, ch], 1)
    for n in range(0, 16, 2):
        squares = []
        for m in range(2):
            t = ctfy[pl.ds(pl.multiple_of((half * 16 + n + m) * 16, 16), 16), :]
            th, tl = split(t * t)
            squares.append(cat([th, th, tl], 0))
        s = jnp.dot(counts3, cat(squares, 1), preferred_element_type=F32)
        s = s.astype(BF16).astype(F32)
        for m in range(2):
            sw[pl.ds(n + m, 64, stride=16), :] = s[:, m * 128 : (m + 1) * 128]

    def weigh(t, acc):
        blocks = []
        for n in range(16):
            p = t * 16 + n
            s = sw[pl.ds(pl.multiple_of(p * 16, 16), 16), :]
            blocks.append((s * depth[pl.ds(plane * 64 + p, 1), :]).astype(BF16))
        table = tab[pl.ds(pl.multiple_of(t * 2048, 2048), 2048), :]
        return acc + jnp.dot(cat(blocks, 1), table, preferred_element_type=F32)

    weight = lax.fori_loop(0, 4, weigh, jnp.zeros((16, 128), F32))
    loads[10].wait()
    den = weight + prior[pl.ds(pl.multiple_of(plane * 32 + half * 16, 16), 16), :] * images_all
    den = cat([den, den], 0)

    def gather(k, part):
        t = g_index(k)
        a_copy(plane, t, k, t).wait_recv()
        return part + abuf[t].astype(F32)

    xbuf[x] = lax.fori_loop(0, NG - 1, gather, own[half])
    each(NX, lambda k: b_copy(x, k).start(), 1)
    each(NX, lambda k: b_copy(lax.rem(x + k, NX), k).wait_recv(), 1)
    fresh = ((xbuf[0] + xbuf[1]) + (xbuf[2] + xbuf[3])) / den

    slot = vol * 2 + half
    fref[...] = encode(fresh)

    @pl.when(mine)
    def _():
        gq[slot] = fref[...]

    def e_send(k):
        dev = (g_index(k) * NX + x, plane)
        return remote(fref, gq.at[slot], e_s.at[k], e_r.at[slot], dev)

    def e_recv(k):
        t = g_index(k)
        dev = source(t)
        at = dev[1] * 2 + lax.rem(t, 2)
        return remote(gq.at[at], gq.at[at], e_s.at[k], e_r.at[at], dev)

    each(NG - 1, lambda k: e_send(k).start())

    @pl.when(jnp.logical_not(mine))
    def _():
        e_send(NG - 1).start()

    weights = jnp.zeros((32, 32), F32)
    list_iota = lax.broadcasted_iota(jnp.int32, (32, 32), 0)
    for j in range(32):
        picked = jnp.where(pose_t[j : j + 1, :] == pose_iota, resp32, 0.0)
        weights = jnp.where(list_iota == j, jnp.sum(picked, axis=0, keepdims=True), weights)
    w_out[...] = weights.T

    each(NG - 1, lambda k: e_recv(k).wait_recv())

    @pl.when(jnp.logical_not(mine))
    def _():
        e_recv(NG - 1).wait_recv()
        e_send(NG - 1).wait_send()

    each(NV, lambda k: d_copy(vol, k).wait_send(), 1)
    each(NX, lambda k: cb_copy(x, k).wait_send(), 1)
    each(NX, lambda k: b_copy(x, k).wait_send(), 1)

    def close(k):
        ca_copy(g, k).wait_send()
        a_copy(y_plane(k), g_index(k), k, g).wait_send()
        e_send(k).wait_send()

    each(NG - 1, close)


def transform_kernel(gq, dft, w_in, w_out, p_out):
    w_out[...] = w_in[...]
    rows = decode(gq[...]).reshape(512, 128)
    gh, gl = split(rows)
    for h in range(2):
        high, low = split(dft[h * 256 : (h + 1) * 256, :])
        p_out[0, :, h * 128 : (h + 1) * 128] = jnp.dot(
            cat([high, low, high], 1), cat([gh, gh, gl], 0), preferred_element_type=F32
        )


def per_device(
    images, volume, ctf_table, ctf_class, pose_list, tilt, offset, magnif, noise_inverse, prior
):
    images_all = float(images.shape[0] * lax.axis_size("img"))
    vmem = pl.BlockSpec(memory_space=pltpu.VMEM)
    limit = 20 * 1024 * 1024
    pinned = [
        pltpu.with_memory_space_constraint(x, pltpu.HBM)
        for x in (
            tilt.reshape(1, -1),
            offset.reshape(1, -1),
            magnif.reshape(1, -1),
            volume,
            images,
            ctf_table,
            ctf_class,
            ctf_class.reshape(1, -1),
            pose_list,
            noise_inverse.reshape(1, -1),
            prior.reshape(256, 128),
        )
    ]
    weights, rows = pl.pallas_call(
        functools.partial(kernel, images_all),
        out_shape=(
            jax.ShapeDtypeStruct((32, 32), F32),
            jax.ShapeDtypeStruct((16, 32, 128), CODE),
        ),
        in_specs=[pl.BlockSpec(memory_space=pltpu.HBM)] * 11,
        out_specs=(vmem, vmem),
        scratch_shapes=[
            pltpu.VMEM((1, 64), F32),
            pltpu.VMEM((1, 64), F32),
            pltpu.VMEM((1, 64), F32),
            pltpu.VMEM((8, 32, 256), BF16),
            pltpu.VMEM((32, 32, 256), BF16),
            pltpu.VMEM((16, 32, 128), F32),
            pltpu.SMEM((32,), jnp.int32),
            pltpu.VMEM((1, 32), jnp.int32),
            pltpu.VMEM((32, 32), jnp.int32),
            pltpu.VMEM((1, 32), F32),
            pltpu.VMEM((256, 128), F32),
            pltpu.VMEM((64, 128), F32),
            pltpu.VMEM((64, 128), F32),
            pltpu.VMEM((512, 128), F32),
            pltpu.VMEM((512, 128), F32),
            pltpu.VMEM((8192, 128), BF16),
            pltpu.VMEM((2, 2048, 128), F32),
            pltpu.VMEM((2, 1024, 128), F32),
            pltpu.VMEM((4096, 128), F32),
            pltpu.VMEM((1024, 128), F32),
            pltpu.VMEM((8, 16, 128), F32),
            pltpu.VMEM((16, 8, 128), F32),
            pltpu.VMEM((4, 8, 128), F32),
            pltpu.VMEM((8, 2, 32, 128), BF16),
            pltpu.VMEM((2, 32, 128), F32),
            pltpu.VMEM((16, 32, 128), BF16),
            pltpu.VMEM((4, 32, 128), F32),
            pltpu.VMEM((32, 128), CODE),
            pltpu.SemaphoreType.DMA((11,)),
        ]
        + [pltpu.SemaphoreType.DMA((8,))] * 2
        + [pltpu.SemaphoreType.DMA((16,))] * 2
        + [pltpu.SemaphoreType.DMA((4,))] * 2
        + [pltpu.SemaphoreType.DMA((16,))] * 2
        + [pltpu.SemaphoreType.DMA((4,))] * 2
        + [pltpu.SemaphoreType.DMA((16,))] * 2,
        compiler_params=pltpu.CompilerParams(
            collective_id=0, has_side_effects=True, vmem_limit_bytes=limit
        ),
    )(*pinned)
    return pl.pallas_call(
        transform_kernel,
        out_shape=(
            jax.ShapeDtypeStruct((32, 32), F32),
            jax.ShapeDtypeStruct((1, 256, 256), F32),
        ),
        in_specs=[vmem] * 3,
        out_specs=(vmem, vmem),
        compiler_params=pltpu.CompilerParams(vmem_limit_bytes=limit),
    )(rows, jnp.asarray(dft_table()), weights)


def solution(mesh):
    placed = (
        P("img", "vol", None),
        P(None, "vol", None),
        P(None, "vol", None),
        P("img"),
        P("img", None),
        P(),
        P(),
        P(),
        P("img"),
        P(None, "vol", None),
    )
    return jax.shard_map(
        per_device,
        mesh=mesh,
        in_specs=placed,
        out_specs=(P("img", None), P("vol", None, None)),
        check_vma=False,
    )
```

time: 636 us -> 54.3 us (0.09)
  blocking collectives: 523 us -> 0 us
  local copies, waits for them, and re-layouts: 73.5 us -> 0.01 us
  Pallas kernels: 0 us -> 53.6 us
  matrix products: 29.7 us -> 0 us
  other arithmetic: 7.11 us -> 0 us
    psum x2 -> x0, blocking collectives: 461 us -> none  [the longest x1 432 us: per_device(): lax.psum(jnp.concatenate([sums.reshape(poses, rows, 2 * cols), jnp.dot(co...]
    all_to_all x1 -> x0, blocking collectives: 62.5 us -> none  [per_device(): lax.all_to_all(fresh, 'vol', split_axis=0, concat_axis=2, tiled=True)]
    pallas_call x0 -> x2, Pallas kernels: none -> 53.6 us  [the longest x1 52.2 us: per_device(): pl.pallas_call(functools.partial(kernel, images_all), out_shape=(jax.Shap...]
    unnamed x82 -> x2, local copies, waits for them, and re-layouts: 32.5 us -> 0.01 us
    dot_general x24 -> x0, matrix products: 29.7 us -> none  [the longest x8 18.1 us: project(): jnp.dot(flat, table, preferred_element_type=jnp.float32)]
    dot_general x8 -> x0, local copies, waits for them, and re-layouts: 21.1 us -> none  [project(): jnp.dot(flat, table, preferred_element_type=jnp.float32)]
    transpose x9 -> x0, local copies, waits for them, and re-layouts: 12.1 us -> none  [project(): jnp.transpose(across[begin:stop], (1, 0, 2)).reshape(cols, size * cols)]
where the time goes in v1:
time: 54.3 us; the launch traced here: 54.2 us
  Pallas kernels  53.6 us (99%)
  between operations  0.66 us (1%)
    pallas_call x1, Pallas kernels, per_device(): pl.pallas_call(functools.partial(kernel, images_all), out_shape=(jax.Shap...  52.2 us
    pallas_call x1, Pallas kernels, per_device(): pl.pallas_call(transform_kernel, out_shape=(jax.ShapeDtypeStruct((32, 32)...  1.35 us

profile of v1, /device:TPU:1, one launch (start us, length us, event | category | flops | bytes accessed | tf_op | source)
XLA Modules:
  0.0 54.2 jit_solution(6126630175628844921)
XLA Ops:
  0.6 0.0 copy-start
  0.6 52.2 %shard_map.122 = (f32[32,32]{1,0:T(8,128)S(1)}, s16[16,32,128]{2,1,0:T(8,128)(2,1)S(1)}) custom-call(f32[1,64]{1,0:T(1,128)} %bitcast.8, f32[1,64]{1,0:T(1,128)} %bitcast.9, f32[1,64]{1,0:T(1,128)} %bitcast.10, bf16[8,32,256]{2,1,0:T(8,128)(2,1)} %volume_h.1, bf16[32,32,256]{2,1,0:T(8,128)(2,1)} %images_h.1, f32[16,32,128]{2,1,0:T(8,128)} %ctf_h.1, ...), custom_call_target="tpu_custom_call" | custom-call | tf_op jit(solution)/shard_map/pallas_call | solution.py:441
  52.9 0.0 copy-done
  52.9 1.3 %shard_map.123 = (f32[32,32]{1,0:T(8,128)}, f32[1,256,256]{2,1,0:T(8,128)}) custom-call(s16[16,32,128]{2,1,0:T(8,128)(2,1)S(1)} %get-tuple-element.4.gq, f32[512,512]{1,0:T(8,128)S(1)} %copy-done, f32[32,32]{1,0:T(8,128)S(1)} %get-tuple-element.5.w_in), custom_call_target="tpu_custom_call" | custom-call | tf_op jit(solution)/shard_map/pallas_call | solution.py:490
Async XLA Ops:
  0.6 52.2 %copy-start = (f32[512,512]{1,0:T(8,128)S(1)}, f32[512,512]{1,0:T(8,128)}, u32[]{:S(2)}) copy-start(f32[512,512]{1,0:T(8,128)} %constant.2.clone.dft) | copy-start | bytes 3145732

commit v2 on v1

--- a/solution.py
+++ b/solution.py
@@ -11,6 +11,7 @@
 NG = 16
 NX = 4
 NV = 8
+FAR = (4, 3, 5, 2, 6, 1, 7, 0)
 F32 = jnp.float32
 BF16 = jnp.bfloat16
 CODE = jnp.int16
@@ -84,18 +85,12 @@
     def vol_peer(k):
         return (img, lax.rem(vol + k, NV))
 
-    def g_index(k):
-        n = k // 2
-        m = (n + 1) // 2
-        offset = 4 + m * (1 - 2 * (n % 2))
-        return lax.rem(a + offset, NY) * 2 + lax.rem(half + 1 - k % 2, 2)
-
-    def each(count, act, start=0):
-        def step(k, carry):
-            act(k)
-            return carry
-
-        lax.fori_loop(start, count, step, 0)
+    near = [half, lax.rem(half + 1, 2)]
+    peers = []
+    for k in FAR:
+        row = lax.rem(a + k, NY) if k else a
+        peers += [(row, near[h], row * 2 + near[h]) for h in (1, 0)]
+    others = peers[:-1]
 
     def g_peer(t):
         return (t * NX + x, vol)
@@ -108,20 +103,21 @@
     def greet(dev):
         pl.semaphore_signal(barrier, inc=1, device_id=dev, device_id_type=pl.DeviceIdType.MESH)
 
-    each(NV, lambda k: greet(vol_peer(k)), 1)
-    each(NX, lambda k: greet(x_peer(lax.rem(x + k, NX))), 1)
-    each(NG - 1, lambda k: greet(g_peer(g_index(k))))
+    for k in range(1, NV):
+        greet(vol_peer(k))
+    for k in range(1, NX):
+        greet(x_peer(lax.rem(x + k, NX)))
+    for row, h, t in others:
+        greet(g_peer(t))
     mine = a == 0
     plane = lax.rem(a + vol, NV)
 
-    def source(t):
-        return (t * NX + x, lax.rem(vol + NV - lax.div(t, 2), NV))
-
-    each(NG - 1, lambda k: greet(source(g_index(k))))
-
-    @pl.when(jnp.logical_not(mine))
-    def _():
-        greet(source(g))
+    def source(row, t):
+        return (t * NX + x, lax.rem(vol + NV - row, NV))
+
+    for row, h, t in others:
+        greet(source(row, t))
+    pl.when(jnp.logical_not(mine))(functools.partial(greet, source(a, g)))
 
     def remote(src, dst, ss, rs, dev):
         return pltpu.make_async_remote_copy(
@@ -219,10 +215,8 @@
 
     pl.semaphore_wait(barrier, 41 - mine.astype(jnp.int32))
 
-    def d_copy(v, k):
-        return remote(dbuf.at[v], dbuf.at[v], d_s.at[k], d_r.at[v], vol_peer(k))
-
-    each(NV, lambda k: d_copy(vol, k).start(), 1)
+    for k in range(1, NV):
+        remote(dbuf.at[vol], dbuf.at[vol], d_s, d_r, vol_peer(k)).start()
 
     def turn(t, carry):
         us = lax.broadcasted_iota(jnp.int32, (128, 128), 0).astype(F32)
@@ -240,7 +234,8 @@
     for j in range(32):
         listed = listed + jnp.where(pose_t[j : j + 1, :] == pose_iota, 1.0, 0.0)
 
-    each(NV, lambda k: d_copy(lax.rem(vol + k, NV), k).wait_recv(), 1)
+    d_all = remote(dbuf.at[0:7], dbuf.at[0:7], d_s, d_r, vol_peer(1))
+    d_all.wait_recv()
     packed = dbuf[0]
     for v in range(1, NV):
         packed = packed + dbuf[v]
@@ -253,19 +248,8 @@
 
     counts = lax.dot_general(resp, hot, NT, preferred_element_type=F32)
     cabuf[g] = cat([counts[8 * n : 8 * n + 8] for n in range(8)], 1)
-    def ca_copy(t, k):
-        return remote(cabuf.at[t], cabuf.at[t], ca_s.at[k], ca_r.at[t], g_peer(g_index(k)))
-
-    def cb_copy(t, k):
-        return remote(cbbuf.at[t], cbbuf.at[t], cb_s.at[k], cb_r.at[t], x_peer(lax.rem(x + k, NX)))
-
-    def a_copy(z, t, k, slot):
-        return remote(vout.at[z, lax.rem(t, 2)], abuf.at[slot], a_s.at[k], a_r.at[slot], g_peer(t))
-
-    def b_copy(t, k):
-        return remote(xbuf.at[t], xbuf.at[t], b_s.at[k], b_r.at[t], x_peer(lax.rem(x + k, NX)))
-
-    each(NG - 1, lambda k: ca_copy(g, k).start())
+    for row, h, t in others:
+        remote(cabuf.at[g], cabuf.at[g], ca_s, ca_r, g_peer(t)).start()
 
     def summing(t, carry):
         for n in range(8):
@@ -296,27 +280,31 @@
 
         return lax.fori_loop(0, 4, body, jnp.zeros((64 * len(planes), 128), F32))
 
-    def y_plane(k):
-        return lax.rem(lax.div(g_index(k), 2) + vol, NV)
-
+    ca_all = remote(cabuf.at[0:15], cabuf.at[0:15], ca_s, ca_r, g_peer(others[0][2]))
+    cb_all = remote(cbbuf.at[0:3], cbbuf.at[0:3], cb_s, cb_r, x_peer(lax.rem(x + 1, NX)))
     for r in range(2):
-        planes = [y_plane(8 * r + 2 * n) for n in range(4)]
+        group = peers[8 * r : 8 * r + 8]
+        planes = [lax.rem(row + vol, NV) for row, h, t in group[::2]]
         acc = back(planes)
         for n, z in enumerate(planes):
             piece = acc[n * 64 : (n + 1) * 64, :].reshape(2, 32, 128)
             vout[z] = piece.astype(BF16)
             if r == 1 and n == 3:
                 own[...] = piece
-        each(8 * r + 8 - r, lambda k: a_copy(y_plane(k), g_index(k), k, g).start(), 8 * r)
+            for row, h, t in group[2 * n : 2 * n + 2]:
+                if t is not peers[-1][2]:
+                    remote(vout.at[z, h], abuf.at[g], a_s, a_r, g_peer(t)).start()
         if r == 0:
-            each(NG - 1, lambda k: ca_copy(g_index(k), k).wait_recv())
+            ca_all.wait_recv()
             total = cabuf[0]
             for t in range(1, NG):
                 total = total + cabuf[t]
             cbbuf[x] = total
-            each(NX, lambda k: cb_copy(x, k).start(), 1)
-
-    each(NX, lambda k: cb_copy(lax.rem(x + k, NX), k).wait_recv(), 1)
+            for k in range(1, NX):
+                dev = x_peer(lax.rem(x + k, NX))
+                remote(cbbuf.at[x], cbbuf.at[x], cb_s, cb_r, dev).start()
+
+    cb_all.wait_recv()
     total = (cbbuf[0] + cbbuf[1]) + (cbbuf[2] + cbbuf[3])
     counts_all = cat([total[:, 16 * n : 16 * n + 16] for n in range(8)], 0)
     ch, cl = split(counts_all)
@@ -346,14 +334,17 @@
     den = weight + prior[pl.ds(pl.multiple_of(plane * 32 + half * 16, 16), 16), :] * images_all
     den = cat([den, den], 0)
 
-    def gather(k, part):
-        t = g_index(k)
-        a_copy(plane, t, k, t).wait_recv()
-        return part + abuf[t].astype(F32)
-
-    xbuf[x] = lax.fori_loop(0, NG - 1, gather, own[half])
-    each(NX, lambda k: b_copy(x, k).start(), 1)
-    each(NX, lambda k: b_copy(lax.rem(x + k, NX), k).wait_recv(), 1)
+    a_all = remote(abuf.at[0:15], abuf.at[0:15], a_s, a_r, g_peer(others[0][2]))
+    a_all.wait_recv()
+    part = own[half]
+    for row, h, t in others:
+        part = part + abuf[t].astype(F32)
+    xbuf[x] = part
+    for k in (2, 1, 3):
+        dev = x_peer(lax.rem(x + k, NX))
+        remote(xbuf.at[x], xbuf.at[x], b_s, b_r, dev).start()
+    b_all = remote(xbuf.at[0:3], xbuf.at[0:3], b_s, b_r, x_peer(lax.rem(x + 1, NX)))
+    b_all.wait_recv()
     fresh = ((xbuf[0] + xbuf[1]) + (xbuf[2] + xbuf[3])) / den
 
     slot = vol * 2 + half
@@ -363,21 +354,9 @@
     def _():
         gq[slot] = fref[...]
 
-    def e_send(k):
-        dev = (g_index(k) * NX + x, plane)
-        return remote(fref, gq.at[slot], e_s.at[k], e_r.at[slot], dev)
-
-    def e_recv(k):
-        t = g_index(k)
-        dev = source(t)
-        at = dev[1] * 2 + lax.rem(t, 2)
-        return remote(gq.at[at], gq.at[at], e_s.at[k], e_r.at[at], dev)
-
-    each(NG - 1, lambda k: e_send(k).start())
-
-    @pl.when(jnp.logical_not(mine))
-    def _():
-        e_send(NG - 1).start()
+    for row, h, t in others:
+        remote(fref, gq.at[slot], e_s, e_r, (t * NX + x, plane)).start()
+    pl.when(jnp.logical_not(mine))(remote(fref, gq.at[slot], e_s, e_r, (img, plane)).start)
 
     weights = jnp.zeros((32, 32), F32)
     list_iota = lax.broadcasted_iota(jnp.int32, (32, 32), 0)
@@ -386,23 +365,16 @@
         weights = jnp.where(list_iota == j, jnp.sum(picked, axis=0, keepdims=True), weights)
     w_out[...] = weights.T
 
-    each(NG - 1, lambda k: e_recv(k).wait_recv())
-
-    @pl.when(jnp.logical_not(mine))
-    def _():
-        e_recv(NG - 1).wait_recv()
-        e_send(NG - 1).wait_send()
-
-    each(NV, lambda k: d_copy(vol, k).wait_send(), 1)
-    each(NX, lambda k: cb_copy(x, k).wait_send(), 1)
-    each(NX, lambda k: b_copy(x, k).wait_send(), 1)
-
-    def close(k):
-        ca_copy(g, k).wait_send()
-        a_copy(y_plane(k), g_index(k), k, g).wait_send()
-        e_send(k).wait_send()
-
-    each(NG - 1, close)
+    for copies in (d_all, ca_all, cb_all, a_all, b_all):
+        copies.wait_send()
+
+    def finish(count):
+        copies = remote(gq.at[0:count], gq.at[0:count], e_s, e_r, g_peer(others[0][2]))
+        copies.wait_recv()
+        copies.wait_send()
+
+    pl.when(mine)(functools.partial(finish, NG - 1))
+    pl.when(jnp.logical_not(mine))(functools.partial(finish, NG))
 
 
 def transform_kernel(gq, dft, w_in, w_out, p_out):
@@ -477,12 +449,7 @@
             pltpu.VMEM((32, 128), CODE),
             pltpu.SemaphoreType.DMA((11,)),
         ]
-        + [pltpu.SemaphoreType.DMA((8,))] * 2
-        + [pltpu.SemaphoreType.DMA((16,))] * 2
-        + [pltpu.SemaphoreType.DMA((4,))] * 2
-        + [pltpu.SemaphoreType.DMA((16,))] * 2
-        + [pltpu.SemaphoreType.DMA((4,))] * 2
-        + [pltpu.SemaphoreType.DMA((16,))] * 2,
+        + [pltpu.SemaphoreType.DMA] * 12,
         compiler_params=pltpu.CompilerParams(
             collective_id=0, has_side_effects=True, vmem_limit_bytes=limit
         ),

time: 54.3 us -> 52.3 us (0.963)
  Pallas kernels: 53.6 us -> 51.5 us
    pallas_call x1, Pallas kernels: 52.2 us -> 50.2 us  [per_device(): pl.pallas_call(functools.partial(kernel, images_all), out_shape=(jax.Shap...]
where the time goes in v2:
time: 52.3 us; the launch traced here: 52.2 us
  Pallas kernels  51.5 us (98%)
  between operations  0.66 us (1%)
    pallas_call x1, Pallas kernels, per_device(): pl.pallas_call(functools.partial(kernel, images_all), out_shape=(jax.Shap...  50.2 us
    pallas_call x1, Pallas kernels, per_device(): pl.pallas_call(transform_kernel, out_shape=(jax.ShapeDtypeStruct((32, 32)...  1.35 us

profile of v2, /device:TPU:1, one launch (start us, length us, event | category | flops | bytes accessed | tf_op | source)
XLA Modules:
  0.0 52.2 jit_solution(10604891259923682485)
XLA Ops:
  0.6 0.0 copy-start
  0.6 50.2 %shard_map.122 = (f32[32,32]{1,0:T(8,128)S(1)}, s16[16,32,128]{2,1,0:T(8,128)(2,1)S(1)}) custom-call(f32[1,64]{1,0:T(1,128)} %bitcast.8, f32[1,64]{1,0:T(1,128)} %bitcast.9, f32[1,64]{1,0:T(1,128)} %bitcast.10, bf16[8,32,256]{2,1,0:T(8,128)(2,1)} %volume_h.1, bf16[32,32,256]{2,1,0:T(8,128)(2,1)} %images_h.1, f32[16,32,128]{2,1,0:T(8,128)} %ctf_h.1, ...), custom_call_target="tpu_custom_call" | custom-call | tf_op jit(solution)/shard_map/pallas_call | solution.py:413
  50.8 0.0 copy-done
  50.9 1.4 %shard_map.123 = (f32[32,32]{1,0:T(8,128)}, f32[1,256,256]{2,1,0:T(8,128)}) custom-call(s16[16,32,128]{2,1,0:T(8,128)(2,1)S(1)} %get-tuple-element.4.gq, f32[512,512]{1,0:T(8,128)S(1)} %copy-done, f32[32,32]{1,0:T(8,128)S(1)} %get-tuple-element.5.w_in), custom_call_target="tpu_custom_call" | custom-call | tf_op jit(solution)/shard_map/pallas_call | solution.py:457
Async XLA Ops:
  0.6 50.2 %copy-start = (f32[512,512]{1,0:T(8,128)S(1)}, f32[512,512]{1,0:T(8,128)}, u32[]{:S(2)}) copy-start(f32[512,512]{1,0:T(8,128)} %constant.2.clone.dft) | copy-start | bytes 3145732

commit v3 on v2

--- a/solution.py
+++ b/solution.py
@@ -112,13 +112,6 @@
     mine = a == 0
     plane = lax.rem(a + vol, NV)
 
-    def source(row, t):
-        return (t * NX + x, lax.rem(vol + NV - row, NV))
-
-    for row, h, t in others:
-        greet(source(row, t))
-    pl.when(jnp.logical_not(mine))(functools.partial(greet, source(a, g)))
-
     def remote(src, dst, ss, rs, dev):
         return pltpu.make_async_remote_copy(
             src_ref=src, dst_ref=dst, send_sem=ss, recv_sem=rs, device_id=dev,
@@ -135,7 +128,8 @@
     for z in range(8):
         depth[z * 64 : (z + 1) * 64, :] = jnp.maximum(0.0, 1.0 - jnp.abs(float(z) - sz))
 
-    loads[3].wait()
+    for load in loads[3:10]:
+        load.wait()
 
     def project_pair(j):
         xs = lax.broadcasted_iota(jnp.int32, (128, 128), 0).astype(F32)
@@ -160,26 +154,19 @@
             for h in range(2):
                 sl[c, pl.ds(2 * j + h, 32, stride=64), :] = slab[:, h * 128 : (h + 1) * 128]
 
+    def filtering(i):
+        own_ctf = ctf[cls_s[i]]
+        for c in range(2):
+            f = images[i, :, c * 128 : (c + 1) * 128].astype(F32) * own_ctf
+            fil[c, pl.ds(i, 32, stride=32), :] = f.astype(BF16).astype(F32)
+
     def project(t, carry):
         for n in range(4):
             project_pair(t * 4 + n)
+            filtering(t * 4 + n)
         return carry
 
     lax.fori_loop(0, 8, project, 0)
-
-    for load in loads[4:10]:
-        load.wait()
-
-    def filtering(t, carry):
-        for n in range(8):
-            i = t * 8 + n
-            own = ctf[cls_s[i]]
-            for c in range(2):
-                f = images[i, :, c * 128 : (c + 1) * 128].astype(F32) * own
-                fil[c, pl.ds(i, 32, stride=32), :] = f.astype(BF16).astype(F32)
-        return carry
-
-    lax.fori_loop(0, 4, filtering, 0)
     for k in range(16):
         ctfy[pl.ds(k, 32, stride=16), :] = ctf[k]
 
@@ -213,7 +200,7 @@
     part = cross - 0.5 * norm_img
     dbuf[vol] = cat([part[16 * g : 16 * g + 16] for g in range(4)], 1)
 
-    pl.semaphore_wait(barrier, 41 - mine.astype(jnp.int32))
+    pl.semaphore_wait(barrier, 25)
 
     for k in range(1, NV):
         remote(dbuf.at[vol], dbuf.at[vol], d_s, d_r, vol_peer(k)).start()
@@ -251,20 +238,12 @@
     for row, h, t in others:
         remote(cabuf.at[g], cabuf.at[g], ca_s, ca_r, g_peer(t)).start()
 
-    def summing(t, carry):
-        for n in range(8):
-            y = t * 8 + n
-            f = cat(
-                [fil[c, pl.ds(pl.multiple_of(y * 32, 32), 32), :].astype(BF16) for c in range(2)],
-                1,
-            )
-            s = jnp.dot(resp, f, preferred_element_type=F32)
-            row = lax.div(t, 2) * 32 + lax.rem(t, 2) * 8 + n
-            for c in range(2):
-                sums[pl.ds(row + 16 * c, 64, stride=64), :] = s[:, c * 128 : (c + 1) * 128]
-        return carry
-
-    lax.fori_loop(0, 4, summing, 0)
+    for y in range(32):
+        f = cat([fil[c, y * 32 : (y + 1) * 32, :].astype(BF16) for c in range(2)], 1)
+        s = jnp.dot(resp, f, preferred_element_type=F32)
+        row = (y // 16) * 32 + y % 16
+        for c in range(2):
+            sums[pl.ds(row + 16 * c, 64, stride=64), :] = s[:, c * 128 : (c + 1) * 128]
 
     def back(planes):
         def body(t, acc):

time: 52.3 us -> 53 us (1.013)
  Pallas kernels: 51.5 us -> 52.2 us
    pallas_call x1, Pallas kernels: 50.2 us -> 50.9 us  [per_device(): pl.pallas_call(functools.partial(kernel, images_all), out_shape=(jax.Shap...]
where the time goes in v3:
time: 53 us; the launch traced here: 52.9 us
  Pallas kernels  52.2 us (98%)
  between operations  0.66 us (1%)
    pallas_call x1, Pallas kernels, per_device(): pl.pallas_call(functools.partial(kernel, images_all), out_shape=(jax.Shap...  50.9 us
    pallas_call x1, Pallas kernels, per_device(): pl.pallas_call(transform_kernel, out_shape=(jax.ShapeDtypeStruct((32, 32)...  1.35 us

profile of v3, /device:TPU:1, one launch (start us, length us, event | category | flops | bytes accessed | tf_op | source)
XLA Modules:
  0.0 52.9 jit_solution(17544363579863496185)
XLA Ops:
  0.6 0.0 copy-start
  0.6 50.9 %shard_map.122 = (f32[32,32]{1,0:T(8,128)S(1)}, s16[16,32,128]{2,1,0:T(8,128)(2,1)S(1)}) custom-call(f32[1,64]{1,0:T(1,128)} %bitcast.8, f32[1,64]{1,0:T(1,128)} %bitcast.9, f32[1,64]{1,0:T(1,128)} %bitcast.10, bf16[8,32,256]{2,1,0:T(8,128)(2,1)} %volume_h.1, bf16[32,32,256]{2,1,0:T(8,128)(2,1)} %images_h.1, f32[16,32,128]{2,1,0:T(8,128)} %ctf_h.1, ...), custom_call_target="tpu_custom_call" | custom-call | tf_op jit(solution)/shard_map/pallas_call | solution.py:392
  51.5 0.0 copy-done
  51.5 1.4 %shard_map.123 = (f32[32,32]{1,0:T(8,128)}, f32[1,256,256]{2,1,0:T(8,128)}) custom-call(s16[16,32,128]{2,1,0:T(8,128)(2,1)S(1)} %get-tuple-element.4.gq, f32[512,512]{1,0:T(8,128)S(1)} %copy-done, f32[32,32]{1,0:T(8,128)S(1)} %get-tuple-element.5.w_in), custom_call_target="tpu_custom_call" | custom-call | tf_op jit(solution)/shard_map/pallas_call | solution.py:436
Async XLA Ops:
  0.6 50.9 %copy-start = (f32[512,512]{1,0:T(8,128)S(1)}, f32[512,512]{1,0:T(8,128)}, u32[]{:S(2)}) copy-start(f32[512,512]{1,0:T(8,128)} %constant.2.clone.dft) | copy-start | bytes 3145732

commit v4 on v2

--- a/solution.py
+++ b/solution.py
@@ -10,6 +10,7 @@
 NY = 8
 NG = 16
 NX = 4
+NQ = 8
 NV = 8
 FAR = (4, 3, 5, 2, 6, 1, 7, 0)
 F32 = jnp.float32
@@ -58,9 +59,9 @@
 
 def kernel(
     images_all,
-    tilt_h, offset_h, magnif_h, volume_h, images_h, ctf_h, cls_h, cls_row_h, poses_h, noise_h, prior_h,
-    w_out, gq,
-    tilt_v, offset_v, magnif_v, volume, images, ctf, cls_s, cls_v, poses_v, noise_v, prior,
+    tilt_h, offset_h, magnif_h, volume_h, images_h, ctf_h, cls_h, cls_row_h, poses_h, noise_h, prior_h, dft_h,
+    w_out, gq, turns,
+    tilt_v, offset_v, magnif_v, volume, images, ctf, cls_s, cls_v, poses_v, noise_v, prior, dft,
     ap, sx, depth, ctfy, tab, sl, fil, sums, sw,
     dbuf, cabuf, cbbuf, vout, own, abuf, xbuf, fref,
     load_sem, d_s, d_r, ca_s, ca_r, cb_s, cb_r, a_s, a_r, b_s, b_r, e_s, e_r,
@@ -75,7 +76,7 @@
             [
                 (tilt_h, tilt_v), (offset_h, offset_v), (magnif_h, magnif_v), (volume_h, volume),
                 (images_h, images), (ctf_h, ctf), (cls_h, cls_s), (cls_row_h, cls_v),
-                (poses_h, poses_v), (noise_h, noise_v), (prior_h, prior),
+                (poses_h, poses_v), (noise_h, noise_v), (prior_h, prior), (dft_h, dft),
             ]
         )
     ]
@@ -98,6 +99,9 @@
     def x_peer(t):
         return (g * NX + t, vol)
 
+    def h_peer(h, t):
+        return (a * NQ + h * NX + t, vol)
+
     barrier = pltpu.get_barrier_semaphore()
 
     def greet(dev):
@@ -106,18 +110,12 @@
     for k in range(1, NV):
         greet(vol_peer(k))
     for k in range(1, NX):
-        greet(x_peer(lax.rem(x + k, NX)))
+        for h in near:
+            greet(h_peer(h, lax.rem(x + k, NX)))
     for row, h, t in others:
         greet(g_peer(t))
     mine = a == 0
     plane = lax.rem(a + vol, NV)
-
-    def source(row, t):
-        return (t * NX + x, lax.rem(vol + NV - row, NV))
-
-    for row, h, t in others:
-        greet(source(row, t))
-    pl.when(jnp.logical_not(mine))(functools.partial(greet, source(a, g)))
 
     def remote(src, dst, ss, rs, dev):
         return pltpu.make_async_remote_copy(
@@ -213,7 +211,7 @@
     part = cross - 0.5 * norm_img
     dbuf[vol] = cat([part[16 * g : 16 * g + 16] for g in range(4)], 1)
 
-    pl.semaphore_wait(barrier, 41 - mine.astype(jnp.int32))
+    pl.semaphore_wait(barrier, 28)
 
     for k in range(1, NV):
         remote(dbuf.at[vol], dbuf.at[vol], d_s, d_r, vol_peer(k)).start()
@@ -247,9 +245,9 @@
     resp = resp32.astype(BF16)
 
     counts = lax.dot_general(resp, hot, NT, preferred_element_type=F32)
-    cabuf[g] = cat([counts[8 * n : 8 * n + 8] for n in range(8)], 1)
-    for row, h, t in others:
-        remote(cabuf.at[g], cabuf.at[g], ca_s, ca_r, g_peer(t)).start()
+    cabuf[a] = cat([counts[8 * n : 8 * n + 8] for n in range(8)], 1)
+    for row, h, t in peers[1:-1:2]:
+        remote(cabuf.at[a], cabuf.at[a], ca_s, ca_r, g_peer(t)).start()
 
     def summing(t, carry):
         for n in range(8):
@@ -280,8 +278,8 @@
 
         return lax.fori_loop(0, 4, body, jnp.zeros((64 * len(planes), 128), F32))
 
-    ca_all = remote(cabuf.at[0:15], cabuf.at[0:15], ca_s, ca_r, g_peer(others[0][2]))
-    cb_all = remote(cbbuf.at[0:3], cbbuf.at[0:3], cb_s, cb_r, x_peer(lax.rem(x + 1, NX)))
+    ca_all = remote(cabuf.at[0:7], cabuf.at[0:7], ca_s, ca_r, g_peer(others[0][2]))
+    cb_all = remote(cbbuf.at[0:7], cbbuf.at[0:7], cb_s, cb_r, x_peer(lax.rem(x + 1, NX)))
     for r in range(2):
         group = peers[8 * r : 8 * r + 8]
         planes = [lax.rem(row + vol, NV) for row, h, t in group[::2]]
@@ -297,15 +295,21 @@
         if r == 0:
             ca_all.wait_recv()
             total = cabuf[0]
-            for t in range(1, NG):
+            for t in range(1, NY):
                 total = total + cabuf[t]
-            cbbuf[x] = total
-            for k in range(1, NX):
-                dev = x_peer(lax.rem(x + k, NX))
-                remote(cbbuf.at[x], cbbuf.at[x], cb_s, cb_r, dev).start()
+            spot = half * NX + x
+            cbbuf[spot] = total
+            for k in (2, 1, 3, 0):
+                for h in near[::-1]:
+                    if k == 0 and h is near[0]:
+                        continue
+                    dev = h_peer(h, lax.rem(x + k, NX) if k else x)
+                    remote(cbbuf.at[spot], cbbuf.at[spot], cb_s, cb_r, dev).start()
 
     cb_all.wait_recv()
-    total = (cbbuf[0] + cbbuf[1]) + (cbbuf[2] + cbbuf[3])
+    total = cbbuf[0]
+    for t in range(1, NQ):
+        total = total + cbbuf[t]
     counts_all = cat([total[:, 16 * n : 16 * n + 16] for n in range(8)], 0)
     ch, cl = split(counts_all)
     counts3 = cat([ch, cl, ch], 1)
@@ -320,20 +324,6 @@
         for m in range(2):
             sw[pl.ds(n + m, 64, stride=16), :] = s[:, m * 128 : (m + 1) * 128]
 
-    def weigh(t, acc):
-        blocks = []
-        for n in range(16):
-            p = t * 16 + n
-            s = sw[pl.ds(pl.multiple_of(p * 16, 16), 16), :]
-            blocks.append((s * depth[pl.ds(plane * 64 + p, 1), :]).astype(BF16))
-        table = tab[pl.ds(pl.multiple_of(t * 2048, 2048), 2048), :]
-        return acc + jnp.dot(cat(blocks, 1), table, preferred_element_type=F32)
-
-    weight = lax.fori_loop(0, 4, weigh, jnp.zeros((16, 128), F32))
-    loads[10].wait()
-    den = weight + prior[pl.ds(pl.multiple_of(plane * 32 + half * 16, 16), 16), :] * images_all
-    den = cat([den, den], 0)
-
     a_all = remote(abuf.at[0:15], abuf.at[0:15], a_s, a_r, g_peer(others[0][2]))
     a_all.wait_recv()
     part = own[half]
@@ -343,6 +333,21 @@
     for k in (2, 1, 3):
         dev = x_peer(lax.rem(x + k, NX))
         remote(xbuf.at[x], xbuf.at[x], b_s, b_r, dev).start()
+
+    def weigh(t, acc):
+        blocks = []
+        for n in range(16):
+            p = t * 16 + n
+            s = sw[pl.ds(pl.multiple_of(p * 16, 16), 16), :]
+            blocks.append((s * depth[pl.ds(plane * 64 + p, 1), :]).astype(BF16))
+        table = tab[pl.ds(pl.multiple_of(t * 2048, 2048), 2048), :]
+        return acc + jnp.dot(cat(blocks, 1), table, preferred_element_type=F32)
+
+    weight = lax.fori_loop(0, 4, weigh, jnp.zeros((16, 128), F32))
+    loads[10].wait()
+    den = weight + prior[pl.ds(pl.multiple_of(plane * 32 + half * 16, 16), 16), :] * images_all
+    den = cat([den, den], 0)
+
     b_all = remote(xbuf.at[0:3], xbuf.at[0:3], b_s, b_r, x_peer(lax.rem(x + 1, NX)))
     b_all.wait_recv()
     fresh = ((xbuf[0] + xbuf[1]) + (xbuf[2] + xbuf[3])) / den
@@ -364,6 +369,14 @@
         picked = jnp.where(pose_t[j : j + 1, :] == pose_iota, resp32, 0.0)
         weights = jnp.where(list_iota == j, jnp.sum(picked, axis=0, keepdims=True), weights)
     w_out[...] = weights.T
+    loads[11].wait()
+
+    def divide(t, carry):
+        at = pl.ds(pl.multiple_of(t * 64, 64), 64)
+        turns[at, 0:512], turns[at, 512:1024] = split(dft[at, :])
+        return carry
+
+    lax.fori_loop(0, 8, divide, 0)
 
     for copies in (d_all, ca_all, cb_all, a_all, b_all):
         copies.wait_send()
@@ -377,14 +390,14 @@
     pl.when(jnp.logical_not(mine))(functools.partial(finish, NG))
 
 
-def transform_kernel(gq, dft, w_in, w_out, p_out):
+def transform_kernel(gq, turns, w_in, w_out, p_out):
     w_out[...] = w_in[...]
-    rows = decode(gq[...]).reshape(512, 128)
-    gh, gl = split(rows)
+    gh, gl = split(decode(gq[...]).reshape(512, 128))
+    rows = cat([gh, gh, gl], 0)
     for h in range(2):
-        high, low = split(dft[h * 256 : (h + 1) * 256, :])
+        both = turns[h * 256 : (h + 1) * 256, :]
         p_out[0, :, h * 128 : (h + 1) * 128] = jnp.dot(
-            cat([high, low, high], 1), cat([gh, gh, gl], 0), preferred_element_type=F32
+            cat([both, both[:, 0:512]], 1), rows, preferred_element_type=F32
         )
 
 
@@ -408,16 +421,18 @@
             pose_list,
             noise_inverse.reshape(1, -1),
             prior.reshape(256, 128),
+            jnp.asarray(dft_table()),
         )
     ]
-    weights, rows = pl.pallas_call(
+    weights, rows, turns = pl.pallas_call(
         functools.partial(kernel, images_all),
         out_shape=(
             jax.ShapeDtypeStruct((32, 32), F32),
             jax.ShapeDtypeStruct((16, 32, 128), CODE),
+            jax.ShapeDtypeStruct((512, 1024), BF16),
         ),
-        in_specs=[pl.BlockSpec(memory_space=pltpu.HBM)] * 11,
-        out_specs=(vmem, vmem),
+        in_specs=[pl.BlockSpec(memory_space=pltpu.HBM)] * 12,
+        out_specs=(vmem, vmem, vmem),
         scratch_shapes=[
             pltpu.VMEM((1, 64), F32),
             pltpu.VMEM((1, 64), F32),
@@ -430,6 +445,7 @@
             pltpu.VMEM((32, 32), jnp.int32),
             pltpu.VMEM((1, 32), F32),
             pltpu.VMEM((256, 128), F32),
+            pltpu.VMEM((512, 512), F32),
             pltpu.VMEM((64, 128), F32),
             pltpu.VMEM((64, 128), F32),
             pltpu.VMEM((512, 128), F32),
@@ -440,14 +456,14 @@
             pltpu.VMEM((4096, 128), F32),
             pltpu.VMEM((1024, 128), F32),
             pltpu.VMEM((8, 16, 128), F32),
-            pltpu.VMEM((16, 8, 128), F32),
-            pltpu.VMEM((4, 8, 128), F32),
+            pltpu.VMEM((8, 8, 128), F32),
+            pltpu.VMEM((8, 8, 128), F32),
             pltpu.VMEM((8, 2, 32, 128), BF16),
             pltpu.VMEM((2, 32, 128), F32),
             pltpu.VMEM((16, 32, 128), BF16),
             pltpu.VMEM((4, 32, 128), F32),
             pltpu.VMEM((32, 128), CODE),
-            pltpu.SemaphoreType.DMA((11,)),
+            pltpu.SemaphoreType.DMA((12,)),
         ]
         + [pltpu.SemaphoreType.DMA] * 12,
         compiler_params=pltpu.CompilerParams(
@@ -463,7 +479,7 @@
         in_specs=[vmem] * 3,
         out_specs=(vmem, vmem),
         compiler_params=pltpu.CompilerParams(vmem_limit_bytes=limit),
-    )(rows, jnp.asarray(dft_table()), weights)
+    )(rows, turns, weights)
 
 
 def solution(mesh):

time: 52.3 us -> 48.3 us (0.924)
  Pallas kernels: 51.5 us -> 47.5 us
    pallas_call x1, Pallas kernels: 50.2 us -> 46.1 us  [per_device(): pl.pallas_call(functools.partial(kernel, images_all), out_shape=(jax.Shap...]
where the time goes in v4:
time: 48.3 us; the launch traced here: 48.1 us
  Pallas kernels  47.5 us (98%)
  between operations  0.64 us (1%)
    pallas_call x1, Pallas kernels, per_device(): pl.pallas_call(functools.partial(kernel, images_all), out_shape=(jax.Shap...  46.1 us
    pallas_call x1, Pallas kernels, per_device(): pl.pallas_call(transform_kernel, out_shape=(jax.ShapeDtypeStruct((32, 32)...  1.35 us

profile of v4, /device:TPU:1, one launch (start us, length us, event | category | flops | bytes accessed | tf_op | source)
XLA Modules:
  0.0 48.1 jit_solution(13643247588070388404)
XLA Ops:
  0.6 46.1 %shard_map.122 = (f32[32,32]{1,0:T(8,128)S(1)}, s16[16,32,128]{2,1,0:T(8,128)(2,1)S(1)}, bf16[512,1024]{1,0:T(8,128)(2,1)S(1)}) custom-call(f32[1,64]{1,0:T(1,128)} %bitcast.8, f32[1,64]{1,0:T(1,128)} %bitcast.9, f32[1,64]{1,0:T(1,128)} %bitcast.10, bf16[8,32,256]{2,1,0:T(8,128)(2,1)} %volume_h.1, bf16[32,32,256]{2,1,0:T(8,128)(2,1)} %images_h.1, ...), custom_call_target="tpu_custom_call" | custom-call | tf_op jit(solution)/shard_map/pallas_call | solution.py:427
  46.8 1.4 %shard_map.123 = (f32[32,32]{1,0:T(8,128)}, f32[1,256,256]{2,1,0:T(8,128)}) custom-call(s16[16,32,128]{2,1,0:T(8,128)(2,1)S(1)} %get-tuple-element.5.gq, bf16[512,1024]{1,0:T(8,128)(2,1)S(1)} %get-tuple-element.6.turns, f32[32,32]{1,0:T(8,128)S(1)} %get-tuple-element.7.w_in), custom_call_target="tpu_custom_call" | custom-call | tf_op jit(solution)/shard_map/pallas_call | solution.py:473

commit v5 on v4

--- a/solution.py
+++ b/solution.py
@@ -245,9 +245,14 @@
     resp = resp32.astype(BF16)
 
     counts = lax.dot_general(resp, hot, NT, preferred_element_type=F32)
-    cabuf[a] = cat([counts[8 * n : 8 * n + 8] for n in range(8)], 1)
-    for row, h, t in peers[1:-1:2]:
-        remote(cabuf.at[a], cabuf.at[a], ca_s, ca_r, g_peer(t)).start()
+    spot = half * NX + x
+    cabuf[spot] = cat([counts[8 * n : 8 * n + 8] for n in range(8)], 1)
+    for k in (2, 1, 3, 0):
+        for h in near[::-1]:
+            if k == 0 and h is near[0]:
+                continue
+            dev = h_peer(h, lax.rem(x + k, NX) if k else x)
+            remote(cabuf.at[spot], cabuf.at[spot], ca_s, ca_r, dev).start()
 
     def summing(t, carry):
         for n in range(8):
@@ -264,51 +269,45 @@
 
     lax.fori_loop(0, 4, summing, 0)
 
-    def back(planes):
+    def back(h):
         def body(t, acc):
             blocks = []
             for n in range(16):
                 p = t * 16 + n
-                s = sums[pl.ds(pl.multiple_of(p * 64, 64), 64), :]
+                s = sums[pl.ds(pl.multiple_of(p * 64 + h * 32, 32), 32), :]
                 blocks.append(
-                    cat([(s * depth[pl.ds(z * 64 + p, 1), :]).astype(BF16) for z in planes], 0)
+                    cat([(s * depth[pl.ds(z * 64 + p, 1), :]).astype(BF16) for z in range(8)], 0)
                 )
             table = tab[pl.ds(pl.multiple_of(t * 2048, 2048), 2048), :]
             return acc + jnp.dot(cat(blocks, 1), table, preferred_element_type=F32)
 
-        return lax.fori_loop(0, 4, body, jnp.zeros((64 * len(planes), 128), F32))
+        return lax.fori_loop(0, 4, body, jnp.zeros((256, 128), F32)).reshape(8, 32, 128)
 
     ca_all = remote(cabuf.at[0:7], cabuf.at[0:7], ca_s, ca_r, g_peer(others[0][2]))
-    cb_all = remote(cbbuf.at[0:7], cbbuf.at[0:7], cb_s, cb_r, x_peer(lax.rem(x + 1, NX)))
-    for r in range(2):
-        group = peers[8 * r : 8 * r + 8]
-        planes = [lax.rem(row + vol, NV) for row, h, t in group[::2]]
-        acc = back(planes)
-        for n, z in enumerate(planes):
-            piece = acc[n * 64 : (n + 1) * 64, :].reshape(2, 32, 128)
-            vout[z] = piece.astype(BF16)
-            if r == 1 and n == 3:
-                own[...] = piece
-            for row, h, t in group[2 * n : 2 * n + 2]:
-                if t is not peers[-1][2]:
-                    remote(vout.at[z, h], abuf.at[g], a_s, a_r, g_peer(t)).start()
-        if r == 0:
-            ca_all.wait_recv()
-            total = cabuf[0]
-            for t in range(1, NY):
-                total = total + cabuf[t]
-            spot = half * NX + x
-            cbbuf[spot] = total
-            for k in (2, 1, 3, 0):
-                for h in near[::-1]:
-                    if k == 0 and h is near[0]:
-                        continue
-                    dev = h_peer(h, lax.rem(x + k, NX) if k else x)
-                    remote(cbbuf.at[spot], cbbuf.at[spot], cb_s, cb_r, dev).start()
+    cb_all = remote(cbbuf.at[0:7], cbbuf.at[0:7], cb_s, cb_r, g_peer(others[0][2]))
+
+    vout[0] = back(near[1]).astype(BF16)
+    for row, h, t in peers[0::2]:
+        z = lax.rem(row + vol, NV)
+        remote(vout.at[0, z], abuf.at[g], a_s, a_r, g_peer(t)).start()
+
+    ca_all.wait_recv()
+    total = cabuf[0]
+    for t in range(1, NQ):
+        total = total + cabuf[t]
+    cbbuf[a] = total
+    for row, h, t in peers[1:-1:2]:
+        remote(cbbuf.at[a], cbbuf.at[a], cb_s, cb_r, g_peer(t)).start()
+
+    own[...] = back(half)
+    vout[1] = own[...].astype(BF16)
+    for row, h, t in peers[1:-1:2]:
+        z = lax.rem(row + vol, NV)
+        remote(vout.at[1, z], abuf.at[g], a_s, a_r, g_peer(t)).start()
 
     cb_all.wait_recv()
     total = cbbuf[0]
-    for t in range(1, NQ):
+    for t in range(1, NY):
         total = total + cbbuf[t]
     counts_all = cat([total[:, 16 * n : 16 * n + 16] for n in range(8)], 0)
     ch, cl = split(counts_all)
@@ -326,7 +325,7 @@
 
     a_all = remote(abuf.at[0:15], abuf.at[0:15], a_s, a_r, g_peer(others[0][2]))
     a_all.wait_recv()
-    part = own[half]
+    part = own[plane]
     for row, h, t in others:
         part = part + abuf[t].astype(F32)
     xbuf[x] = part
@@ -458,8 +457,8 @@
             pltpu.VMEM((8, 16, 128), F32),
             pltpu.VMEM((8, 8, 128), F32),
             pltpu.VMEM((8, 8, 128), F32),
-            pltpu.VMEM((8, 2, 32, 128), BF16),
-            pltpu.VMEM((2, 32, 128), F32),
+            pltpu.VMEM((2, 8, 32, 128), BF16),
+            pltpu.VMEM((8, 32, 128), F32),
             pltpu.VMEM((16, 32, 128), BF16),
             pltpu.VMEM((4, 32, 128), F32),
             pltpu.VMEM((32, 128), CODE),

time: 48.3 us -> 47.9 us (level)
  no operation moved by 1% of the time
where the time goes in v5:
time: 47.9 us; the launch traced here: 47.7 us
  Pallas kernels  47.1 us (98%)
  between operations  0.64 us (1%)
    pallas_call x1, Pallas kernels, per_device(): pl.pallas_call(functools.partial(kernel, images_all), out_shape=(jax.Shap...  45.7 us
    pallas_call x1, Pallas kernels, per_device(): pl.pallas_call(transform_kernel, out_shape=(jax.ShapeDtypeStruct((32, 32)...  1.35 us

profile of v5, /device:TPU:1, one launch (start us, length us, event | category | flops | bytes accessed | tf_op | source)
XLA Modules:
  0.0 47.7 jit_solution(8554583797338578299)
XLA Ops:
  0.6 45.7 %shard_map.122 = (f32[32,32]{1,0:T(8,128)S(1)}, s16[16,32,128]{2,1,0:T(8,128)(2,1)S(1)}, bf16[512,1024]{1,0:T(8,128)(2,1)S(1)}) custom-call(f32[1,64]{1,0:T(1,128)} %bitcast.8, f32[1,64]{1,0:T(1,128)} %bitcast.9, f32[1,64]{1,0:T(1,128)} %bitcast.10, bf16[8,32,256]{2,1,0:T(8,128)(2,1)} %volume_h.1, bf16[32,32,256]{2,1,0:T(8,128)(2,1)} %images_h.1, ...), custom_call_target="tpu_custom_call" | custom-call | tf_op jit(solution)/shard_map/pallas_call | solution.py:426
  46.4 1.3 %shard_map.123 = (f32[32,32]{1,0:T(8,128)}, f32[1,256,256]{2,1,0:T(8,128)}) custom-call(s16[16,32,128]{2,1,0:T(8,128)(2,1)S(1)} %get-tuple-element.5.gq, bf16[512,1024]{1,0:T(8,128)(2,1)S(1)} %get-tuple-element.6.turns, f32[32,32]{1,0:T(8,128)S(1)} %get-tuple-element.7.w_in), custom_call_target="tpu_custom_call" | custom-call | tf_op jit(solution)/shard_map/pallas_call | solution.py:472

commit v6 on v5

--- a/solution.py
+++ b/solution.py
@@ -114,8 +114,12 @@
             greet(h_peer(h, lax.rem(x + k, NX)))
     for row, h, t in others:
         greet(g_peer(t))
-    mine = a == 0
-    plane = lax.rem(a + vol, NV)
+    def partner(row):
+        chip = lax.rem(lax.div(row, 2) + 4 - lax.div(vol, 2), 4)
+        return chip * 2 + lax.rem(row + vol, 2)
+
+    plane = partner(a)
+    mine = plane == vol
 
     def remote(src, dst, ss, rs, dev):
         return pltpu.make_async_remote_copy(
@@ -288,7 +292,7 @@
 
     vout[0] = back(near[1]).astype(BF16)
     for row, h, t in peers[0::2]:
-        z = lax.rem(row + vol, NV)
+        z = partner(row)
         remote(vout.at[0, z], abuf.at[g], a_s, a_r, g_peer(t)).start()
 
     ca_all.wait_recv()
@@ -302,7 +306,7 @@
     own[...] = back(half)
     vout[1] = own[...].astype(BF16)
     for row, h, t in peers[1:-1:2]:
-        z = lax.rem(row + vol, NV)
+        z = partner(row)
         remote(vout.at[1, z], abuf.at[g], a_s, a_r, g_peer(t)).start()
 
     cb_all.wait_recv()

time: 47.9 us -> 47.9 us (level)
  no operation moved by 1% of the time
where the time goes in v6:
time: 47.9 us; the launch traced here: 47.7 us
  Pallas kernels  47.1 us (98%)
  between operations  0.64 us (1%)
    pallas_call x1, Pallas kernels, per_device(): pl.pallas_call(functools.partial(kernel, images_all), out_shape=(jax.Shap...  45.7 us
    pallas_call x1, Pallas kernels, per_device(): pl.pallas_call(transform_kernel, out_shape=(jax.ShapeDtypeStruct((32, 32)...  1.35 us

profile of v6, /device:TPU:1, one launch (start us, length us, event | category | flops | bytes accessed | tf_op | source)
XLA Modules:
  0.0 47.7 jit_solution(513924394953814862)
XLA Ops:
  0.6 45.7 %shard_map.122 = (f32[32,32]{1,0:T(8,128)S(1)}, s16[16,32,128]{2,1,0:T(8,128)(2,1)S(1)}, bf16[512,1024]{1,0:T(8,128)(2,1)S(1)}) custom-call(f32[1,64]{1,0:T(1,128)} %bitcast.8, f32[1,64]{1,0:T(1,128)} %bitcast.9, f32[1,64]{1,0:T(1,128)} %bitcast.10, bf16[8,32,256]{2,1,0:T(8,128)(2,1)} %volume_h.1, bf16[32,32,256]{2,1,0:T(8,128)(2,1)} %images_h.1, ...), custom_call_target="tpu_custom_call" | custom-call | tf_op jit(solution)/shard_map/pallas_call | solution.py:430
  46.4 1.3 %shard_map.123 = (f32[32,32]{1,0:T(8,128)}, f32[1,256,256]{2,1,0:T(8,128)}) custom-call(s16[16,32,128]{2,1,0:T(8,128)(2,1)S(1)} %get-tuple-element.5.gq, bf16[512,1024]{1,0:T(8,128)(2,1)S(1)} %get-tuple-element.6.turns, f32[32,32]{1,0:T(8,128)S(1)} %get-tuple-element.7.w_in), custom_call_target="tpu_custom_call" | custom-call | tf_op jit(solution)/shard_map/pallas_call | solution.py:476

commit v7 on v6

--- a/solution.py
+++ b/solution.py
@@ -13,6 +13,7 @@
 NQ = 8
 NV = 8
 FAR = (4, 3, 5, 2, 6, 1, 7, 0)
+ROWS, ROWS_I, ROWS_K = 72, 40, 24
 F32 = jnp.float32
 BF16 = jnp.bfloat16
 CODE = jnp.int16
@@ -160,7 +161,7 @@
             odd = jnp.where(on[1], s[1], jnp.where(on[3], s[3], jnp.where(on[5], s[5], s[7])))
             slab = (even * even_w + odd * odd_w).astype(BF16).astype(F32)
             for h in range(2):
-                sl[c, pl.ds(2 * j + h, 32, stride=64), :] = slab[:, h * 128 : (h + 1) * 128]
+                sl[c, pl.ds(2 * j + h, 32, stride=ROWS), :] = slab[:, h * 128 : (h + 1) * 128]
 
     def project(t, carry):
         for n in range(4):
@@ -178,12 +179,12 @@
             own = ctf[cls_s[i]]
             for c in range(2):
                 f = images[i, :, c * 128 : (c + 1) * 128].astype(F32) * own
-                fil[c, pl.ds(i, 32, stride=32), :] = f.astype(BF16).astype(F32)
+                fil[c, pl.ds(i, 32, stride=ROWS_I), :] = f.astype(BF16).astype(F32)
         return carry
 
     lax.fori_loop(0, 4, filtering, 0)
     for k in range(16):
-        ctfy[pl.ds(k, 32, stride=16), :] = ctf[k]
+        ctfy[pl.ds(k, 32, stride=ROWS_K), :] = ctf[k]
 
     def scoring(g, carry):
         cross, norm = carry
@@ -192,11 +193,11 @@
             y = g * 8 + n
             power = None
             for c in range(2):
-                lhs.append(fil[c, pl.ds(pl.multiple_of(y * 32, 32), 32), :].astype(BF16))
-                s = sl[c, pl.ds(pl.multiple_of(y * 64, 64), 64), :]
+                lhs.append(fil[c, pl.ds(pl.multiple_of(y * ROWS_I, 8), 32), :].astype(BF16))
+                s = sl[c, pl.ds(pl.multiple_of(y * ROWS, 8), 64), :]
                 rhs.append(s.astype(BF16))
                 power = s * s if power is None else power + s * s
-            t = ctfy[pl.ds(pl.multiple_of(y * 16, 16), 16), :]
+            t = ctfy[pl.ds(pl.multiple_of(y * ROWS_K, 8), 16), :]
             th, tl = split(t * t)
             ph, plo = split(power)
             nl += [th, tl, th]
@@ -262,13 +263,13 @@
         for n in range(8):
             y = t * 8 + n
             f = cat(
-                [fil[c, pl.ds(pl.multiple_of(y * 32, 32), 32), :].astype(BF16) for c in range(2)],
+                [fil[c, pl.ds(pl.multiple_of(y * ROWS_I, 8), 32), :].astype(BF16) for c in range(2)],
                 1,
             )
             s = jnp.dot(resp, f, preferred_element_type=F32)
             row = lax.div(t, 2) * 32 + lax.rem(t, 2) * 8 + n
             for c in range(2):
-                sums[pl.ds(row + 16 * c, 64, stride=64), :] = s[:, c * 128 : (c + 1) * 128]
+                sums[pl.ds(row + 16 * c, 64, stride=ROWS), :] = s[:, c * 128 : (c + 1) * 128]
         return carry
 
     lax.fori_loop(0, 4, summing, 0)
@@ -278,7 +279,7 @@
             blocks = []
             for n in range(16):
                 p = t * 16 + n
-                s = sums[pl.ds(pl.multiple_of(p * 64 + h * 32, 32), 32), :]
+                s = sums[pl.ds(pl.multiple_of(p * ROWS + h * 32, 8), 32), :]
                 blocks.append(
                     cat([(s * depth[pl.ds(z * 64 + p, 1), :]).astype(BF16) for z in range(8)], 0)
                 )
@@ -319,13 +320,13 @@
     for n in range(0, 16, 2):
         squares = []
         for m in range(2):
-            t = ctfy[pl.ds(pl.multiple_of((half * 16 + n + m) * 16, 16), 16), :]
+            t = ctfy[pl.ds(pl.multiple_of((half * 16 + n + m) * ROWS_K, 8), 16), :]
             th, tl = split(t * t)
             squares.append(cat([th, th, tl], 0))
         s = jnp.dot(counts3, cat(squares, 1), preferred_element_type=F32)
         s = s.astype(BF16).astype(F32)
         for m in range(2):
-            sw[pl.ds(n + m, 64, stride=16), :] = s[:, m * 128 : (m + 1) * 128]
+            sw[pl.ds(n + m, 64, stride=ROWS_K), :] = s[:, m * 128 : (m + 1) * 128]
 
     a_all = remote(abuf.at[0:15], abuf.at[0:15], a_s, a_r, g_peer(others[0][2]))
     a_all.wait_recv()
@@ -341,7 +342,7 @@
         blocks = []
         for n in range(16):
             p = t * 16 + n
-            s = sw[pl.ds(pl.multiple_of(p * 16, 16), 16), :]
+            s = sw[pl.ds(pl.multiple_of(p * ROWS_K, 8), 16), :]
             blocks.append((s * depth[pl.ds(plane * 64 + p, 1), :]).astype(BF16))
         table = tab[pl.ds(pl.multiple_of(t * 2048, 2048), 2048), :]
         return acc + jnp.dot(cat(blocks, 1), table, preferred_element_type=F32)
@@ -452,12 +453,12 @@
             pltpu.VMEM((64, 128), F32),
             pltpu.VMEM((64, 128), F32),
             pltpu.VMEM((512, 128), F32),
-            pltpu.VMEM((512, 128), F32),
+            pltpu.VMEM((32 * ROWS_K, 128), F32),
             pltpu.VMEM((8192, 128), BF16),
-            pltpu.VMEM((2, 2048, 128), F32),
-            pltpu.VMEM((2, 1024, 128), F32),
-            pltpu.VMEM((4096, 128), F32),
-            pltpu.VMEM((1024, 128), F32),
+            pltpu.VMEM((2, 32 * ROWS, 128), F32),
+            pltpu.VMEM((2, 32 * ROWS_I, 128), F32),
+            pltpu.VMEM((64 * ROWS, 128), F32),
+            pltpu.VMEM((64 * ROWS_K, 128), F32),
             pltpu.VMEM((8, 16, 128), F32),
             pltpu.VMEM((8, 8, 128), F32),
             pltpu.VMEM((8, 8, 128), F32),

time: 47.9 us -> 45.5 us (0.950)
  Pallas kernels: 47.1 us -> 44.7 us
    pallas_call x1, Pallas kernels: 45.7 us -> 43.3 us  [per_device(): pl.pallas_call(functools.partial(kernel, images_all), out_shape=(jax.Shap...]
where the time goes in v7:
time: 45.5 us; the launch traced here: 45.3 us
  Pallas kernels  44.7 us (98%)
  between operations  0.64 us (1%)
    pallas_call x1, Pallas kernels, per_device(): pl.pallas_call(functools.partial(kernel, images_all), out_shape=(jax.Shap...  43.3 us
    pallas_call x1, Pallas kernels, per_device(): pl.pallas_call(transform_kernel, out_shape=(jax.ShapeDtypeStruct((32, 32)...  1.35 us

profile of v7, /device:TPU:1, one launch (start us, length us, event | category | flops | bytes accessed | tf_op | source)
XLA Modules:
  0.0 45.3 jit_solution(7359013604276073325)
XLA Ops:
  0.6 43.3 %shard_map.122 = (f32[32,32]{1,0:T(8,128)S(1)}, s16[16,32,128]{2,1,0:T(8,128)(2,1)S(1)}, bf16[512,1024]{1,0:T(8,128)(2,1)S(1)}) custom-call(f32[1,64]{1,0:T(1,128)} %bitcast.8, f32[1,64]{1,0:T(1,128)} %bitcast.9, f32[1,64]{1,0:T(1,128)} %bitcast.10, bf16[8,32,256]{2,1,0:T(8,128)(2,1)} %volume_h.1, bf16[32,32,256]{2,1,0:T(8,128)(2,1)} %images_h.1, ...), custom_call_target="tpu_custom_call" | custom-call | tf_op jit(solution)/shard_map/pallas_call | solution.py:431
  44.0 1.4 %shard_map.123 = (f32[32,32]{1,0:T(8,128)}, f32[1,256,256]{2,1,0:T(8,128)}) custom-call(s16[16,32,128]{2,1,0:T(8,128)(2,1)S(1)} %get-tuple-element.5.gq, bf16[512,1024]{1,0:T(8,128)(2,1)S(1)} %get-tuple-element.6.turns, f32[32,32]{1,0:T(8,128)S(1)} %get-tuple-element.7.w_in), custom_call_target="tpu_custom_call" | custom-call | tf_op jit(solution)/shard_map/pallas_call | solution.py:477

commit v8 on v7

--- a/solution.py
+++ b/solution.py
@@ -138,7 +138,8 @@
     for z in range(8):
         depth[z * 64 : (z + 1) * 64, :] = jnp.maximum(0.0, 1.0 - jnp.abs(float(z) - sz))
 
-    loads[3].wait()
+    for load in loads[3:10]:
+        load.wait()
 
     def project_pair(j):
         xs = lax.broadcasted_iota(jnp.int32, (128, 128), 0).astype(F32)
@@ -163,26 +164,19 @@
             for h in range(2):
                 sl[c, pl.ds(2 * j + h, 32, stride=ROWS), :] = slab[:, h * 128 : (h + 1) * 128]
 
+    def filtering(i):
+        own_ctf = ctf[cls_s[i]]
+        for c in range(2):
+            f = images[i, :, c * 128 : (c + 1) * 128].astype(F32) * own_ctf
+            fil[c, pl.ds(i, 32, stride=ROWS_I), :] = f.astype(BF16).astype(F32)
+
     def project(t, carry):
         for n in range(4):
             project_pair(t * 4 + n)
+            filtering(t * 4 + n)
         return carry
 
     lax.fori_loop(0, 8, project, 0)
-
-    for load in loads[4:10]:
-        load.wait()
-
-    def filtering(t, carry):
-        for n in range(8):
-            i = t * 8 + n
-            own = ctf[cls_s[i]]
-            for c in range(2):
-                f = images[i, :, c * 128 : (c + 1) * 128].astype(F32) * own
-                fil[c, pl.ds(i, 32, stride=ROWS_I), :] = f.astype(BF16).astype(F32)
-        return carry
-
-    lax.fori_loop(0, 4, filtering, 0)
     for k in range(16):
         ctfy[pl.ds(k, 32, stride=ROWS_K), :] = ctf[k]
 
@@ -260,19 +254,19 @@
             remote(cabuf.at[spot], cabuf.at[spot], ca_s, ca_r, dev).start()
 
     def summing(t, carry):
-        for n in range(8):
-            y = t * 8 + n
+        for n in range(16):
+            y = t * 16 + n
             f = cat(
                 [fil[c, pl.ds(pl.multiple_of(y * ROWS_I, 8), 32), :].astype(BF16) for c in range(2)],
                 1,
             )
             s = jnp.dot(resp, f, preferred_element_type=F32)
-            row = lax.div(t, 2) * 32 + lax.rem(t, 2) * 8 + n
+            row = t * 32 + n
             for c in range(2):
                 sums[pl.ds(row + 16 * c, 64, stride=ROWS), :] = s[:, c * 128 : (c + 1) * 128]
         return carry
 
-    lax.fori_loop(0, 4, summing, 0)
+    lax.fori_loop(0, 2, summing, 0)
 
     def back(h):
         def body(t, acc):

time: 45.5 us -> 45.7 us (level)
  no operation moved by 1% of the time
where the time goes in v8:
time: 45.7 us; the launch traced here: 45.6 us
  Pallas kernels  45 us (98%)
  between operations  0.64 us (1%)
    pallas_call x1, Pallas kernels, per_device(): pl.pallas_call(functools.partial(kernel, images_all), out_shape=(jax.Shap...  43.6 us
    pallas_call x1, Pallas kernels, per_device(): pl.pallas_call(transform_kernel, out_shape=(jax.ShapeDtypeStruct((32, 32)...  1.35 us

profile of v8, /device:TPU:1, one launch (start us, length us, event | category | flops | bytes accessed | tf_op | source)
XLA Modules:
  0.0 45.6 jit_solution(9492910958422324865)
XLA Ops:
  0.6 43.6 %shard_map.122 = (f32[32,32]{1,0:T(8,128)S(1)}, s16[16,32,128]{2,1,0:T(8,128)(2,1)S(1)}, bf16[512,1024]{1,0:T(8,128)(2,1)S(1)}) custom-call(f32[1,64]{1,0:T(1,128)} %bitcast.8, f32[1,64]{1,0:T(1,128)} %bitcast.9, f32[1,64]{1,0:T(1,128)} %bitcast.10, bf16[8,32,256]{2,1,0:T(8,128)(2,1)} %volume_h.1, bf16[32,32,256]{2,1,0:T(8,128)(2,1)} %images_h.1, ...), custom_call_target="tpu_custom_call" | custom-call | tf_op jit(solution)/shard_map/pallas_call | solution.py:425
  44.2 1.3 %shard_map.123 = (f32[32,32]{1,0:T(8,128)}, f32[1,256,256]{2,1,0:T(8,128)}) custom-call(s16[16,32,128]{2,1,0:T(8,128)(2,1)S(1)} %get-tuple-element.5.gq, bf16[512,1024]{1,0:T(8,128)(2,1)S(1)} %get-tuple-element.6.turns, f32[32,32]{1,0:T(8,128)S(1)} %get-tuple-element.7.w_in), custom_call_target="tpu_custom_call" | custom-call | tf_op jit(solution)/shard_map/pallas_call | solution.py:471

commit v9 on v7

--- a/solution.py
+++ b/solution.py
@@ -164,11 +164,11 @@
                 sl[c, pl.ds(2 * j + h, 32, stride=ROWS), :] = slab[:, h * 128 : (h + 1) * 128]
 
     def project(t, carry):
-        for n in range(4):
-            project_pair(t * 4 + n)
+        for n in range(8):
+            project_pair(t * 8 + n)
         return carry
 
-    lax.fori_loop(0, 8, project, 0)
+    lax.fori_loop(0, 4, project, 0)
 
     for load in loads[4:10]:
         load.wait()

time: 45.5 us -> 44.9 us (0.987)
  Pallas kernels: 44.7 us -> 44.1 us
    pallas_call x1, Pallas kernels: 43.3 us -> 42.7 us  [per_device(): pl.pallas_call(functools.partial(kernel, images_all), out_shape=(jax.Shap...]
where the time goes in v9:
time: 44.9 us; the launch traced here: 44.7 us
  Pallas kernels  44.1 us (98%)
  between operations  0.64 us (1%)
    pallas_call x1, Pallas kernels, per_device(): pl.pallas_call(functools.partial(kernel, images_all), out_shape=(jax.Shap...  42.7 us
    pallas_call x1, Pallas kernels, per_device(): pl.pallas_call(transform_kernel, out_shape=(jax.ShapeDtypeStruct((32, 32)...  1.35 us

profile of v9, /device:TPU:1, one launch (start us, length us, event | category | flops | bytes accessed | tf_op | source)
XLA Modules:
  0.0 44.7 jit_solution(12792181320389626482)
XLA Ops:
  0.6 42.7 %shard_map.122 = (f32[32,32]{1,0:T(8,128)S(1)}, s16[16,32,128]{2,1,0:T(8,128)(2,1)S(1)}, bf16[512,1024]{1,0:T(8,128)(2,1)S(1)}) custom-call(f32[1,64]{1,0:T(1,128)} %bitcast.8, f32[1,64]{1,0:T(1,128)} %bitcast.9, f32[1,64]{1,0:T(1,128)} %bitcast.10, bf16[8,32,256]{2,1,0:T(8,128)(2,1)} %volume_h.1, bf16[32,32,256]{2,1,0:T(8,128)(2,1)} %images_h.1, ...), custom_call_target="tpu_custom_call" | custom-call | tf_op jit(solution)/shard_map/pallas_call | solution.py:431
  43.4 1.4 %shard_map.123 = (f32[32,32]{1,0:T(8,128)}, f32[1,256,256]{2,1,0:T(8,128)}) custom-call(s16[16,32,128]{2,1,0:T(8,128)(2,1)S(1)} %get-tuple-element.5.gq, bf16[512,1024]{1,0:T(8,128)(2,1)S(1)} %get-tuple-element.6.turns, f32[32,32]{1,0:T(8,128)S(1)} %get-tuple-element.7.w_in), custom_call_target="tpu_custom_call" | custom-call | tf_op jit(solution)/shard_map/pallas_call | solution.py:477
